TPU v7x, 32 devices: a whole 2x2x4 slice. The times are simulated.
32 devices in a mesh: prompt: 2 (over y), wide: 16 (over z, x, core).
Axes of the slice: x: 2, y: 2, z: 4, core: 2. Of those that a mesh axis runs over, the one named last changes fastest.
Arguments:
- candidate_hidden: bfloat16 [2, 2048, 4096], P('prompt', 'wide'), may hold values from -6 to 6
- frozen_query: bfloat16 [2, 2048, 4096], P('prompt', 'wide'), may hold values from -12 to 12
- candidate_key_value: bfloat16 [2, 2048, 2048], P('prompt', 'wide'), may hold values from -6 to 6
- prompt_key_value: bfloat16 [2, 1024, 2048], P('prompt', 'wide'), may hold values from -12 to 12
- candidate_adapter: int32 [2, 16], P('prompt'), may hold values from 0 to 15
- prompt_block_end: int32 [2, 16], P('prompt', 'wide'), may hold values from 1 to 8, as said below
- adapter_down: bfloat16 [16, 4, 16, 4096], P(None, None, None, 'wide'), may hold values from -0.09375 to 0.09375
- adapter_up: bfloat16 [16, 2, 16, 4096], P(None, None, None, 'wide'), may hold values from -0.625 to 0.625
- adapter_up_key_value: bfloat16 [16, 2, 16, 1024], P(None, None, None, 'wide'), may hold values from -0.625 to 0.625
- output_cotangent: bfloat16 [2, 2048, 4096], P('prompt', 'wide'), may hold values from -0.03125 to 0.03125
- context_cotangent: bfloat16 [2, 2048, 4096], P('prompt', 'wide'), may hold values from -0.03125 to 0.03125
Outputs:
- down_gradient: float32 [16, 4, 16, 4096], P(None, None, None, 'wide')
- up_gradient: float32 [16, 2, 16, 4096], P(None, None, None, 'wide')
- key_value_up_gradient: float32 [16, 2, 16, 1024], P(None, None, None, 'wide')
Inputs may be any that keep to these rules, and one draw needn't show every extreme that they name: `prompt_block_end`: the first block of every group sees the whole prompt.
All inputs are finite; a program needn't handle non-finite values.
Results may differ from a plain program's by a relative error of at most 0.02.
Values may be sent and summed in bfloat16 or wider, within the bound.
A program may use at most 192 MiB of HBM per device.

v0:
```python
import jax
import jax.numpy as jnp
from jax import lax
from jax.sharding import PartitionSpec as P

HEADS = 32
KV_HEADS = 8
HEAD_DIM = 128
ADAPTER_COUNT = 16
BLOCK_TOKENS = 128


adapter_scale = 2.0
masked_score = -1e30


def split_heads(rows):
    return rows.reshape(rows.shape[0], KV_HEADS, HEADS // KV_HEADS, HEAD_DIM)


def score_rows(query_vectors, key_rows, visible):
    key_heads = key_rows.reshape(key_rows.shape[0], KV_HEADS, HEAD_DIM)
    scores = jnp.einsum(
        "bkgd,jkd->kgbj", split_heads(query_vectors), key_heads, preferred_element_type=jnp.float32
    ) * HEAD_DIM ** (-0.5)
    return jnp.where(visible, scores, masked_score)


def forward_update(row_peak, row_total, weighted, query_vectors, key_rows, value_rows, visible):
    scores = score_rows(query_vectors, key_rows, visible)
    new_peak = jnp.maximum(row_peak, jnp.max(scores, axis=-1))
    exponent = jnp.where(visible, jnp.exp(scores - new_peak[..., None]), 0.0)
    rescale = jnp.exp(row_peak - new_peak)
    value_heads = value_rows.reshape(value_rows.shape[0], KV_HEADS, HEAD_DIM)
    increment = jnp.einsum(
        "kgbj,jkd->bkgd",
        exponent.astype(jnp.bfloat16),
        value_heads,
        preferred_element_type=jnp.float32,
    )
    weighted = weighted * jnp.transpose(rescale, (2, 0, 1))[..., None] + increment
    row_total = row_total * rescale + jnp.sum(exponent, axis=-1)
    return (new_peak, row_total, weighted)


def backward_terms(
    query_vectors, key_rows, value_rows, visible, row_peak, row_total, context_grad, row_delta
):
    scores = score_rows(query_vectors, key_rows, visible)
    attention = (
        jnp.where(visible, jnp.exp(scores - row_peak[..., None]), 0.0) / row_total[..., None]
    )
    value_heads = value_rows.reshape(value_rows.shape[0], KV_HEADS, HEAD_DIM)
    attention_grad = jnp.einsum(
        "bkgd,jkd->kgbj", split_heads(context_grad), value_heads, preferred_element_type=jnp.float32
    )
    score_grad = (attention * (attention_grad - row_delta[..., None])).astype(jnp.bfloat16)
    return (attention, score_grad)


def body(
    candidate_hidden,
    frozen_query,
    candidate_key_value,
    prompt_key_value,
    candidate_adapter,
    prompt_block_end,
    adapter_down,
    adapter_up,
    adapter_up_key_value,
    output_cotangent,
    context_cotangent,
):
    position = lax.axis_index("wide")
    candidate_blocks = prompt_block_end.shape[1]
    model_width = candidate_hidden.shape[2]
    key_value_width = KV_HEADS * HEAD_DIM
    head_groups = HEADS // KV_HEADS
    inverse_root = HEAD_DIM ** (-0.5)
    group_ids = candidate_adapter[0]
    own_ids = lax.dynamic_slice_in_dim(group_ids, position * candidate_blocks, candidate_blocks)
    whole_a, whole_b, whole_pairs = (
        lax.all_gather(adapter_down, "wide", axis=3, tiled=True),
        lax.all_gather(adapter_up, "wide", axis=3, tiled=True),
        lax.all_gather(adapter_up_key_value, "wide", axis=3, tiled=True),
    )
    down_matrices = whole_a[own_ids]
    up_model_matrix = whole_b[own_ids]
    up_matrix_pairs = whole_pairs[own_ids]
    x_blocks = candidate_hidden[0].reshape(candidate_blocks, BLOCK_TOKENS, model_width)
    rank_projection = jnp.einsum(
        "cbd,cprd->cprb", x_blocks, down_matrices[:, :3], preferred_element_type=jnp.float32
    ).astype(jnp.bfloat16)
    query_adapter_delta = jnp.einsum(
        "crb,crd->cbd",
        rank_projection[:, 0],
        up_model_matrix[:, 0],
        preferred_element_type=jnp.float32,
    )
    query_vectors = (
        frozen_query[0].reshape(candidate_blocks, BLOCK_TOKENS, model_width).astype(jnp.float32)
        + adapter_scale * query_adapter_delta
    ).astype(jnp.bfloat16)
    key_value_delta = jnp.einsum(
        "cprb,cprd->cbpd",
        rank_projection[:, 1:],
        up_matrix_pairs,
        preferred_element_type=jnp.float32,
    ).reshape(candidate_blocks, BLOCK_TOKENS, 2 * key_value_width)
    candidate_own_key_value = (
        candidate_key_value[0]
        .reshape(candidate_blocks, BLOCK_TOKENS, 2 * key_value_width)
        .astype(jnp.float32)
        + adapter_scale * key_value_delta
    ).astype(jnp.bfloat16)
    limits = prompt_block_end[0] * BLOCK_TOKENS
    causal = jnp.arange(BLOCK_TOKENS)[None, :] <= jnp.arange(BLOCK_TOKENS)[:, None]
    start_state = (
        jnp.full(
            (candidate_blocks, KV_HEADS, head_groups, BLOCK_TOKENS), masked_score, jnp.float32
        ),
        jnp.zeros((candidate_blocks, KV_HEADS, head_groups, BLOCK_TOKENS), jnp.float32),
        jnp.zeros((candidate_blocks, BLOCK_TOKENS, KV_HEADS, head_groups, HEAD_DIM), jnp.float32),
    )
    gathered = lax.all_gather(prompt_key_value, "wide", axis=1, tiled=True)
    piece_rows = gathered[0]
    piece_len = piece_rows.shape[0]
    key_position = jnp.arange(piece_len)[None, :]
    peak_list = []
    total_list = []
    weighted_list = []
    block_index = 0
    visible = jnp.broadcast_to(key_position < limits[block_index], (BLOCK_TOKENS, piece_len))
    result = forward_update(
        start_state[0][block_index],
        start_state[1][block_index],
        start_state[2][block_index],
        query_vectors[block_index],
        piece_rows[:, :key_value_width],
        piece_rows[:, key_value_width:],
        visible,
    )
    peak_list.append(result[0])
    total_list.append(result[1])
    weighted_list.append(result[2])
    prompt_state = (jnp.stack(peak_list), jnp.stack(total_list), jnp.stack(weighted_list))
    peak_list, total_list, weighted_list = ([], [], [])
    block_index = 0
    result = forward_update(
        prompt_state[0][block_index],
        prompt_state[1][block_index],
        prompt_state[2][block_index],
        query_vectors[block_index],
        candidate_own_key_value[block_index][:, :key_value_width],
        candidate_own_key_value[block_index][:, key_value_width:],
        causal,
    )
    peak_list.append(result[0])
    total_list.append(result[1])
    weighted_list.append(result[2])
    final_peak = jnp.stack(peak_list)
    final_total = jnp.stack(total_list)
    weighted = jnp.stack(weighted_list)
    context = (
        (weighted / jnp.transpose(final_total, (0, 3, 1, 2))[..., None])
        .astype(jnp.bfloat16)
        .reshape(candidate_blocks, BLOCK_TOKENS, model_width)
    )
    output_gradients = output_cotangent[0].reshape(candidate_blocks, BLOCK_TOKENS, model_width)
    output_rank_rows = jnp.einsum(
        "cbd,crd->crb", context, down_matrices[:, 3], preferred_element_type=jnp.float32
    ).astype(jnp.bfloat16)
    up_output_matrix = (
        adapter_scale
        * jnp.einsum(
            "cbd,crd->crb",
            output_gradients,
            up_model_matrix[:, 1],
            preferred_element_type=jnp.float32,
        )
    ).astype(jnp.bfloat16)
    up_gradient_result = adapter_scale * jnp.einsum(
        "crb,cbd->crd", output_rank_rows, output_gradients, preferred_element_type=jnp.float32
    )
    grad_a_out = jnp.einsum(
        "crb,cbd->crd", up_output_matrix, context, preferred_element_type=jnp.float32
    )
    context_grad = (
        context_cotangent[0]
        .reshape(candidate_blocks, BLOCK_TOKENS, model_width)
        .astype(jnp.float32)
        + jnp.einsum(
            "crb,crd->cbd",
            up_output_matrix,
            down_matrices[:, 3],
            preferred_element_type=jnp.float32,
        )
    ).astype(jnp.bfloat16)
    head_shape = (candidate_blocks, BLOCK_TOKENS, KV_HEADS, head_groups, HEAD_DIM)
    row_delta = jnp.transpose(
        jnp.sum(
            context_grad.astype(jnp.float32).reshape(head_shape)
            * context.astype(jnp.float32).reshape(head_shape),
            axis=-1,
        ),
        (0, 2, 3, 1),
    )
    piece_rows = gathered[0]
    piece_len = piece_rows.shape[0]
    key_position = jnp.arange(piece_len)[None, :]
    key_heads = piece_rows[:, :key_value_width].reshape(piece_len, KV_HEADS, HEAD_DIM)
    block_index = 0
    visible = jnp.broadcast_to(key_position < limits[block_index], (BLOCK_TOKENS, piece_len))
    attention, score_grad = backward_terms(
        query_vectors[block_index],
        piece_rows[:, :key_value_width],
        piece_rows[:, key_value_width:],
        visible,
        final_peak[block_index],
        final_total[block_index],
        context_grad[block_index],
        row_delta[block_index],
    )
    updated = [
        jnp.einsum("kgbj,jkd->bkgd", score_grad, key_heads, preferred_element_type=jnp.float32)
        * inverse_root
    ]
    prompt_grads = jnp.stack(updated)
    query_list, pair_list = ([], [])
    block_index = 0
    own_keys = candidate_own_key_value[block_index][:, :key_value_width]
    attention, score_grad = backward_terms(
        query_vectors[block_index],
        own_keys,
        candidate_own_key_value[block_index][:, key_value_width:],
        causal,
        final_peak[block_index],
        final_total[block_index],
        context_grad[block_index],
        row_delta[block_index],
    )
    own_key_heads = own_keys.reshape(BLOCK_TOKENS, KV_HEADS, HEAD_DIM)
    query_full = (
        prompt_grads[block_index]
        + jnp.einsum(
            "kgbj,jkd->bkgd", score_grad, own_key_heads, preferred_element_type=jnp.float32
        )
        * inverse_root
    )
    query_list.append(query_full.reshape(BLOCK_TOKENS, model_width).astype(jnp.bfloat16))
    key_grad = (
        jnp.einsum(
            "kgbj,bkgd->jkd",
            score_grad,
            split_heads(query_vectors[block_index]),
            preferred_element_type=jnp.float32,
        )
        * inverse_root
    )
    value_grad = jnp.einsum(
        "kgbj,bkgd->jkd",
        attention.astype(jnp.bfloat16),
        split_heads(context_grad[block_index]),
        preferred_element_type=jnp.float32,
    )
    pair_list.append(
        jnp.stack(
            [
                key_grad.reshape(BLOCK_TOKENS, key_value_width),
                value_grad.reshape(BLOCK_TOKENS, key_value_width),
            ],
            axis=1,
        ).astype(jnp.bfloat16)
    )
    query_gradient = jnp.stack(query_list)
    key_value_gradient = jnp.stack(pair_list)
    up_query_matrix = (
        adapter_scale
        * jnp.einsum(
            "cbd,crd->crb",
            query_gradient,
            up_model_matrix[:, 0],
            preferred_element_type=jnp.float32,
        )
    ).astype(jnp.bfloat16)
    up_rank_key_value = (
        adapter_scale
        * jnp.einsum(
            "cbpd,cprd->cprb",
            key_value_gradient,
            up_matrix_pairs,
            preferred_element_type=jnp.float32,
        )
    ).astype(jnp.bfloat16)
    grad_a_qkv = jnp.einsum(
        "cprb,cbd->cprd",
        jnp.concatenate([up_query_matrix[:, None], up_rank_key_value], axis=1),
        x_blocks,
        preferred_element_type=jnp.float32,
    )
    down_gradient = jnp.concatenate([grad_a_qkv, grad_a_out[:, None]], axis=1)
    up_gradient = jnp.stack(
        [
            adapter_scale
            * jnp.einsum(
                "crb,cbd->crd",
                rank_projection[:, 0],
                query_gradient,
                preferred_element_type=jnp.float32,
            ),
            up_gradient_result,
        ],
        axis=1,
    )
    key_value_up_gradient = adapter_scale * jnp.einsum(
        "cprb,cbpd->cprd",
        rank_projection[:, 1:],
        key_value_gradient,
        preferred_element_type=jnp.float32,
    )
    back_a, back_b, back_pairs = (
        lax.all_to_all(
            down_gradient.astype(jnp.bfloat16), "wide", split_axis=3, concat_axis=0, tiled=True
        ).astype(down_gradient.dtype),
        lax.all_to_all(
            up_gradient.astype(jnp.bfloat16), "wide", split_axis=3, concat_axis=0, tiled=True
        ).astype(up_gradient.dtype),
        lax.all_to_all(
            key_value_up_gradient.astype(jnp.bfloat16),
            "wide",
            split_axis=3,
            concat_axis=0,
            tiled=True,
        ).astype(key_value_up_gradient.dtype),
    )
    owners = (group_ids[None, :] == jnp.arange(ADAPTER_COUNT)[:, None]).astype(jnp.float32)
    owned_a = jnp.einsum("ns,sprd->nprd", owners, back_a, precision=lax.Precision.HIGHEST)
    owned_b = jnp.einsum("ns,sprd->nprd", owners, back_b, precision=lax.Precision.HIGHEST)
    owned_pairs = jnp.einsum("ns,sprd->nprd", owners, back_pairs, precision=lax.Precision.HIGHEST)
    total_a, total_b, total_pairs = (
        lax.psum(owned_a.astype(jnp.bfloat16), "prompt").astype(jnp.float32),
        lax.psum(owned_b.astype(jnp.bfloat16), "prompt").astype(jnp.float32),
        lax.psum(owned_pairs.astype(jnp.bfloat16), "prompt").astype(jnp.float32),
    )
    return (total_a, total_b, total_pairs)


def solution(mesh):
    placed = (
        P("prompt", "wide", None),
        P("prompt", "wide", None),
        P("prompt", "wide", None),
        P("prompt", "wide", None),
        P("prompt", None),
        P("prompt", "wide"),
        P(None, None, None, "wide"),
        P(None, None, None, "wide"),
        P(None, None, None, "wide"),
        P("prompt", "wide", None),
        P("prompt", "wide", None),
    )
    return jax.shard_map(
        body,
        mesh=mesh,
        in_specs=placed,
        out_specs=(
            P(None, None, None, "wide"),
            P(None, None, None, "wide"),
            P(None, None, None, "wide"),
        ),
        check_vma=False,
    )
```

profile of v0, /device:TPU:24, one launch (start us, length us, event | category | flops | bytes accessed | tf_op | source)
XLA Modules:
  0.0 443.5 jit_solution(2724692249208814416)
XLA Ops:
  7.2 2.5 copy.89
  16.1 68.8 %all-gather.11.cloned.1.call-done = bf16[16,2,16,1024]{2,0,1,3:T(8,128)(2,1)} async-done(((bf16[16,2,16,64]{2,0,1,3:T(8,128)(2,1)}), bf16[16,2,16,1024]{2,0,1,3:T(8,128)(2,1)}) %all-gather.11.cloned.1.call-update) | async-done | bytes 1048592 | tf_op jit(solution)/shard_map/all_gather | solution.py:85
  84.9 3.3 constant_dynamic-slice_fusion
  89.5 46.6 %all-gather.9.cloned.1.call-done = bf16[1,1024,2048]{2,1,0:T(8,128)(2,1)} async-done(((bf16[1,64,2048]{2,1,0:T(8,128)(2,1)}), bf16[1,1024,2048]{2,1,0:T(8,128)(2,1)}) %all-gather.9.cloned.1.call-update) | async-done | bytes 4194320 | tf_op jit(solution)/shard_map/all_gather | solution.py:125
  136.2 6.4 %copy.85 = bf16[1,1024,2048]{1,2,0:T(8,128)(2,1)} copy(bf16[1,1024,2048]{2,1,0:T(8,128)(2,1)} %all-gather.9.cloned.1.call-done) | data formatting | bytes 8388608 | tf_op jit(solution)/shard_map/all_gather | solution.py:125
  142.6 47.1 %all-gather.5.cloned.1.call-done = bf16[16,2,16,4096]{3,2,1,0:T(8,128)(2,1)} async-done(((bf16[16,2,16,256]{3,2,1,0:T(8,128)(2,1)}), bf16[16,2,16,4096]{3,2,1,0:T(8,128)(2,1)}) %all-gather.5.cloned.1.call-update) | async-done | bytes 4194320 | tf_op jit(solution)/shard_map/all_gather | solution.py:84
  191.0 4.7 %fusion.100 = (bf16[1024,1024]{0,1:T(8,128)(2,1)}, bf16[1024,1024]{0,1:T(8,128)(2,1)}) fusion(bf16[1024,2048]{0,1:T(8,128)(2,1)} %bitcast.306), kind=kLoop, calls=%fused_computation.147 | loop fusion | bytes 8388608 | tf_op jit(solution)/shard_map/slice | solution.py:217
  195.6 72.4 %all-gather.7.cloned.1.call-done = bf16[16,4,16,4096]{3,2,1,0:T(8,128)(2,1)} async-done(((bf16[16,4,16,256]{3,2,1,0:T(8,128)(2,1)}), bf16[16,4,16,4096]{3,2,1,0:T(8,128)(2,1)}) %all-gather.7.cloned.1.call-update) | async-done | bytes 8388624 | tf_op jit(solution)/shard_map/all_gather | solution.py:83
  275.1 2.9 bitcast_reduce_fusion
  278.0 4.7 %fusion.8 = f32[8,4,128]{2,1,0:T(4,128)S(1)} fusion(f32[8,128,4,1024]{3,1,2,0:T(8,128)S(1)} %get-tuple-element.60, f32[8,4,128]{2,1,0:T(4,128)S(1)} %get-tuple-element.57, pred[1024]{0:T(1024)(128)(4,1)S(1)} %iota_compare_fusion.2), kind=kLoop, calls=%fused_computation.13 | loop fusion | flops 20967424 | bytes 16811008 | tf_op jit(solution)/shard_map/reduce_sum | solution.py:42
  289.2 3.6 fusion.36
  292.8 9.0 %multiply_reduce_fusion = (f32[128,8,4]{0,2,1:T(4,128)S(1)}, bf16[128,8,4,128]{0,3,2,1:T(8,128)(2,1)}) fusion(bf16[128,8,4,128]{0,3,2,1:T(8,128)(2,1)S(1)} %bitcast.325, f32[128,8,4]{0,2,1:T(4,128)S(1)} %fusion.63, f32[8,128,4,128]{3,1,2,0:T(8,128)S(1)} %copy-done.8, f32[128,8,4]{0,2,1:T(4,128)S(1)} %get-tuple-element.56, ...), kind=kOutput, calls=%fused_computation.45 | convolution fusion | flops 1099427840 | bytes 23151616 | tf_op jit(solution)/shard_map/kgbj,jkd->bkgd/dot_general | solution.py:35
  303.3 12.9 %fusion.30 = f32[8,4,128,128]{2,3,1,0:T(8,128)} fusion(bf16[1024,8,128,1]{0,2,3,1:T(8,128)(2,1)} %bitcast.307, f32[8,128,4,1024]{3,1,2,0:T(8,128)} %copy-done.1, bf16[128,8,4,128]{0,3,2,1:T(8,128)(2,1)} %bitcast.324, bf16[1024,8,128,1]{0,2,3,1:T(8,128)(2,1)} %bitcast.320, f32[8,4,128]{2,1,0:T(4,128)} %bitcast.334, f32[8,4,128]{2,1,0:T(4,128)S(1)} %multiply_add_fusion, ...), kind=kOutput, calls=%fused_computation.47 | convolution fusion | flops 2181038080 | bytes 24167424 | tf_op jit(solution)/shard_map/kgbj,jkd->bkgd/dot_general | solution.py:225
  322.1 6.3 %all-to-all-start.2 = ((bf16[16,2,1024]{2,1,0:T(2,128)(2,1)}), bf16[16,2,1024]{2,1,0:T(2,128)(2,1)}, u32[]{:S(2)}, u32[]{:S(2)}) async-start(bf16[16,2,1024]{2,1,0:T(2,128)(2,1)} %reshape.439), calls=%async_computation.2 | async-start | bytes 131072 | tf_op jit(solution)/shard_map/all_to_all | solution.py:328
  333.7 3.8 copy.108
  337.5 7.4 %reshape.437 = bf16[16,2,4096]{2,1,0:T(2,128)(2,1)} reshape(bf16[4096,1,2,16]{3,2,1,0:T(2,128)(2,1)} %bitcast.311) | data formatting | bytes 524288
  346.4 6.0 %all-to-all-start.1 = ((bf16[16,2,4096]{2,1,0:T(2,128)(2,1)}), bf16[16,2,4096]{2,1,0:T(2,128)(2,1)S(1)}, u32[]{:S(2)}, u32[]{:S(2)}) async-start(bf16[16,2,4096]{2,1,0:T(2,128)(2,1)} %reshape.437), calls=%async_computation.1 | async-start | bytes 524288 | tf_op jit(solution)/shard_map/all_to_all | solution.py:325
  352.8 4.6 %copy.106 = bf16[1,4,16,4096]{2,1,0,3:T(4,128)(2,1)} copy(bf16[1,4,16,4096]{3,2,1,0:T(8,128)(2,1)S(1)} %pad_maximum_fusion.1) | data formatting | bytes 1048576 | tf_op jit(solution)/shard_map/concatenate | solution.py:301
  357.4 6.4 %reshape.435 = bf16[16,2,8192]{2,1,0:T(2,128)(2,1)} reshape(bf16[4096,1,4,16]{3,2,1,0:T(4,128)(2,1)} %bitcast.304) | data formatting | bytes 1048576
  363.8 6.0 %all-to-all-start = ((bf16[16,2,8192]{2,1,0:T(2,128)(2,1)}), bf16[16,2,8192]{2,1,0:T(2,128)(2,1)}, u32[]{:S(2)}, u32[]{:S(2)}) async-start(bf16[16,2,8192]{2,1,0:T(2,128)(2,1)} %reshape.435), calls=%async_computation | async-start | bytes 1048576 | tf_op jit(solution)/shard_map/all_to_all | solution.py:322
  375.9 6.2 %all-to-all-done = bf16[16,2,8192]{2,1,0:T(2,128)(2,1)} async-done(((bf16[16,2,8192]{2,1,0:T(2,128)(2,1)}), bf16[16,2,8192]{2,1,0:T(2,128)(2,1)}, u32[]{:S(2)}, u32[]{:S(2)}) %all-to-all-start) | async-done | bytes 524320 | tf_op jit(solution)/shard_map/all_to_all | solution.py:322
  382.1 5.4 %reshape.436 = bf16[4096,1,4,16]{3,2,1,0:T(4,128)(2,1)} reshape(bf16[16,2,8192]{2,1,0:T(2,128)(2,1)} %all-to-all-done) | data formatting | bytes 1048576
  387.4 4.6 %copy.138 = bf16[1,4,16,16,256]{4,3,2,1,0:T(8,128)(2,1)S(1)} copy(bf16[1,4,16,16,256]{2,1,4,3,0:T(4,128)(2,1)} %bitcast.305) | data formatting | bytes 1048576 | tf_op jit(solution)/shard_map/all_to_all | solution.py:322
  393.1 39.1 %all-reduce.3.cloned.1.call-done = (bf16[16,4,16,256]{3,0,2,1:T(8,128)(2,1)}, bf16[16,2,16,256]{3,0,2,1:T(8,128)(2,1)}, bf16[16,2,16,64]{3,0,2,1:T(8,128)(2,1)}) async-done(((bf16[16,4,16,256]{3,0,2,1:T(8,128)(2,1)}, bf16[16,2,16,256]{3,0,2,1:T(8,128)(2,1)}, bf16[16,2,16,64]{3,0,2,1:T(8,128)(2,1)}), (bf16[16,4,16,256]{3,0,2,1:T(8,128)(2,1)}, bf16[16,2,16,256]{3,0,2,1:T(8,128)(2,1)}, ...) | async-done | bytes 851984 | tf_op jit(solution)/shard_map/psum | solution.py:341
  (109 shorter events, 46.0 us)
Async XLA Ops:
  7.2 260.8 %copy-start = (bf16[1,128,4096]{2,1,0:T(8,128)(2,1)S(1)}, bf16[1,128,4096]{2,1,0:T(8,128)(2,1)}, u32[]{:S(2)}) copy-start(bf16[1,128,4096]{2,1,0:T(8,128)(2,1)} %param.11) | copy-start | bytes 3145732
  7.2 4.7 %copy-start.23 = (s32[1,16]{1,0:T(1,128)S(1)}, s32[1,16]{1,0:T(1,128)}, u32[]{:S(2)}) copy-start(s32[1,16]{1,0:T(1,128)} %param.15) | copy-start | bytes 196
  7.2 6.6 %copy-start.15 = (bf16[1,128,2048]{2,1,0:T(8,128)(2,1)S(1)}, bf16[1,128,2048]{2,1,0:T(8,128)(2,1)}, u32[]{:S(2)}) copy-start(bf16[1,128,2048]{2,1,0:T(8,128)(2,1)} %param.13) | copy-start | bytes 1572868
  7.2 77.7 %all-gather.11.cloned.1.call-start = ((), (), s32[]{:S(2)}) async-start(), calls=%async_computation.6 | async-start | bytes 8912896 | tf_op jit(solution)/shard_map/all_gather | solution.py:85
  9.8 126.4 %all-gather.9.cloned.1.call-start = ((), (), s32[]{:S(2)}) async-start(), calls=%async_computation.5 | async-start | bytes 4456448 | tf_op jit(solution)/shard_map/all_gather | solution.py:125
  10.5 179.1 %all-gather.5.cloned.1.call-start = ((), (), s32[]{:S(2)}) async-start(), calls=%async_computation.3 | async-start | bytes 4456448 | tf_op jit(solution)/shard_map/all_gather | solution.py:84
  11.3 256.7 %all-gather.7.cloned.1.call-start = ((), (), s32[]{:S(2)}) async-start(), calls=%async_computation.4 | async-start | bytes 8912896 | tf_op jit(solution)/shard_map/all_gather | solution.py:83
  89.5 182.0 %copy-start.16 = (bf16[1,2,16,1024]{3,2,1,0:T(8,128)(2,1)}, bf16[1,2,16,1024]{3,2,1,0:T(8,128)(2,1)S(1)}, u32[]{:S(2)}) copy-start(bf16[1,2,16,1024]{3,2,1,0:T(8,128)(2,1)S(1)} %copy.90) | copy-start | bytes 196612
  89.5 100.2 %copy-start.5 = (bf16[1,128,4096]{2,1,0:T(8,128)(2,1)S(1)}, bf16[1,128,4096]{2,1,0:T(8,128)(2,1)}, u32[]{:S(2)}) copy-start(bf16[1,128,4096]{2,1,0:T(8,128)(2,1)} %param.20) | copy-start | bytes 3145732
  195.6 73.9 %copy-start.10 = (bf16[1,128,4096]{2,1,0:T(8,128)(2,1)S(1)}, bf16[1,128,4096]{2,1,0:T(8,128)(2,1)}, u32[]{:S(2)}) copy-start(bf16[1,128,4096]{2,1,0:T(8,128)(2,1)} %param.12) | copy-start | bytes 3145732
  273.2 11.2 %copy-start.13 = (bf16[128,1024]{0,1:T(8,128)(2,1)}, bf16[128,1024]{0,1:T(8,128)(2,1)S(1)}, u32[]{:S(2)}) copy-start(bf16[128,1024]{0,1:T(8,128)(2,1)S(1)} %get-tuple-element.54) | copy-start | bytes 786436
  273.8 10.7 %copy-start.2 = (f32[8,128,128,4]{2,1,3,0:T(8,128)}, f32[8,128,128,4]{2,1,3,0:T(8,128)S(1)}, u32[]{:S(2)}) copy-start(f32[8,128,128,4]{2,1,3,0:T(8,128)S(1)} %get-tuple-element.62) | copy-start | bytes 6291460
  278.0 5.8 %copy-start.1 = (f32[8,128,4,1024]{3,1,2,0:T(8,128)}, f32[8,128,4,1024]{3,1,2,0:T(8,128)S(1)}, u32[]{:S(2)}) copy-start(f32[8,128,4,1024]{3,1,2,0:T(8,128)S(1)} %get-tuple-element.60) | copy-start | bytes 50331652
  289.2 3.6 copy-start.12
  292.8 9.7 %copy-start.3 = (f32[8,128,128,4]{2,1,3,0:T(8,128)S(1)}, f32[8,128,128,4]{2,1,3,0:T(8,128)}, u32[]{:S(2)}) copy-start(f32[8,128,128,4]{2,1,3,0:T(8,128)} %copy-done.2) | copy-start | bytes 6291460
  292.8 9.7 %copy-start.14 = (bf16[128,1024]{0,1:T(8,128)(2,1)S(1)}, bf16[128,1024]{0,1:T(8,128)(2,1)}, u32[]{:S(2)}) copy-start(bf16[128,1024]{0,1:T(8,128)(2,1)} %copy-done.13) | copy-start | bytes 786436
  322.1 24.2 %all-to-all-start.2 = ((bf16[16,2,1024]{2,1,0:T(2,128)(2,1)}), bf16[16,2,1024]{2,1,0:T(2,128)(2,1)}, u32[]{:S(2)}, u32[]{:S(2)}) async-start(bf16[16,2,1024]{2,1,0:T(2,128)(2,1)} %reshape.439), calls=%async_computation.2 | async-start | bytes 131072 | tf_op jit(solution)/shard_map/all_to_all | solution.py:328
  337.5 8.6 %copy-start.17 = (bf16[1,2,16,1024]{3,2,1,0:T(8,128)(2,1)S(1)}, bf16[1,2,16,1024]{3,2,1,0:T(8,128)(2,1)}, u32[]{:S(2)}) copy-start(bf16[1,2,16,1024]{3,2,1,0:T(8,128)(2,1)} %copy-done.16) | copy-start | bytes 196612
  337.5 8.6 %copy-start.19 = (bf16[128,1,1024]{2,0,1:T(8,128)(2,1)S(1)}, bf16[128,1,1024]{2,0,1:T(8,128)(2,1)}, u32[]{:S(2)}) copy-start(bf16[128,1,1024]{2,0,1:T(8,128)(2,1)} %copy-done.18) | copy-start | bytes 786436
  337.5 8.6 %copy-start.21 = (bf16[128,1,1024]{2,0,1:T(8,128)(2,1)S(1)}, bf16[128,1,1024]{2,0,1:T(8,128)(2,1)}, u32[]{:S(2)}) copy-start(bf16[128,1,1024]{2,0,1:T(8,128)(2,1)} %copy-done.20) | copy-start | bytes 786436
  346.4 17.5 %all-to-all-start.1 = ((bf16[16,2,4096]{2,1,0:T(2,128)(2,1)}), bf16[16,2,4096]{2,1,0:T(2,128)(2,1)S(1)}, u32[]{:S(2)}, u32[]{:S(2)}) async-start(bf16[16,2,4096]{2,1,0:T(2,128)(2,1)} %reshape.437), calls=%async_computation.1 | async-start | bytes 524288 | tf_op jit(solution)/shard_map/all_to_all | solution.py:325
  363.8 18.2 %all-to-all-start = ((bf16[16,2,8192]{2,1,0:T(2,128)(2,1)}), bf16[16,2,8192]{2,1,0:T(2,128)(2,1)}, u32[]{:S(2)}, u32[]{:S(2)}) async-start(bf16[16,2,8192]{2,1,0:T(2,128)(2,1)} %reshape.435), calls=%async_computation | async-start | bytes 1048576 | tf_op jit(solution)/shard_map/all_to_all | solution.py:322
  369.8 62.3 %all-reduce.3.cloned.1.call-start = ((), (), s32[]{:S(2)}) async-start(), calls=%async_computation.7 | async-start | bytes 1835008 | tf_op jit(solution)/shard_map/psum | solution.py:341
  432.2 4.1 copy-start.22
  (9 other events, 17.5 us)
Sparse Core Ops, SparseCore 0:
  10.8 74.0 all-gather.10
  87.1 49.0 all-gather.8
  138.3 51.3 all-gather.4
  191.7 76.2 all-gather.6
  393.2 38.8 all-reduce.2
where the time goes:
time: 446 us; the launch traced here: 443 us
  waiting for transfers between devices  282 us (63%)
  local copies, waits for them, and re-layouts  71.1 us (16%)
  matrix products  48.2 us (11%)
  starting transfers between devices  18.6 us (4%)
  between operations  16.8 us (4%)
  other arithmetic  6.67 us (1%)
    all_gather x1, waiting for transfers between devices, body(): lax.all_gather(adapter_down, 'wide', axis=3, tiled=True)  72.4 us
    all_gather x1, waiting for transfers between devices, body(): lax.all_gather(adapter_up_key_value, 'wide', axis=3, tiled=True)  68.8 us
    all_gather x1, waiting for transfers between devices, body(): lax.all_gather(adapter_up, 'wide', axis=3, tiled=True)  47.1 us
    all_gather x1, waiting for transfers between devices, body(): gathered = lax.all_gather(prompt_key_value, 'wide', axis=1, tiled=True)  46.6 us
    psum x1, waiting for transfers between devices, body(): lax.psum(owned_a.astype(jnp.bfloat16), 'prompt').astype(jnp.float32)  39.1 us
    unnamed x61, local copies, waits for them, and re-layouts  35.6 us
    dot_general x1, matrix products, body(): jnp.einsum('kgbj,jkd->bkgd', score_grad, key_heads, preferred_element_typ...  12.9 us
    dot_general x2, matrix products, forward_update(): jnp.einsum('kgbj,jkd->bkgd', exponent.astype(jnp.bfloat16), value_heads,...  11.1 us
  transfers between devices with their start and end apart: 8, of which 6 were waited for; matrix products, arithmetic and copies ran while one was open for 12% of the time, Pallas kernels for 0%

commit v1 on v0

v1 whole, which is shorter than its diff:
```python
import functools

import jax
import jax.numpy as jnp
from jax import lax
from jax.experimental import pallas as pl
from jax.experimental.pallas import tpu as pltpu
from jax.sharding import PartitionSpec as P

HEADS = 32
KV_HEADS = 8
HEAD_DIM = 128
ADAPTER_COUNT = 16
BLOCK_TOKENS = 128
RANK = 16
HEAD_GROUP = HEADS // KV_HEADS
GROUP_WIDTH = HEAD_GROUP * HEAD_DIM
MESH = pl.DeviceIdType.MESH

adapter_scale = 2.0
masked_score = -1e30
LOG2E = 1.4426950408889634


def dot(a, b, contract=((1,), (0,))):
    return lax.dot_general(a, b, (contract, ((), ())), preferred_element_type=jnp.float32)


NT = ((1,), (1,))
TN = ((0,), (0,))


def chip_at(place, chips):
    place = lax.rem(place + chips, chips)
    return jnp.where(place < chips // 2, 2 * place, 2 * (chips - 1 - place) + 1)


def gather_kernel(n, send_ref, send_pair_ref, prompt_ref, maps_ref, pairs_ref, rows_ref,
                  local_sem, ring_send, ring_recv, core_send, core_recv, part_send, part_recv):
    p = lax.axis_index("prompt")
    w = lax.axis_index("wide")
    chips = n // 2
    half = chips // 2
    core = lax.rem(w, 2)
    chip = w // 2
    place = jnp.where(lax.rem(chip, 2) == 0, chip // 2, chips - 1 - chip // 2)
    rows = prompt_ref.shape[0]
    columns = send_ref.shape[2]
    partner = w + 1 - 2 * core
    ahead = 2 * chip_at(place + 1, chips) + core
    behind = 2 * chip_at(place - 1, chips) + core

    barrier = pltpu.get_barrier_semaphore()
    for k in range(1, n):
        pl.semaphore_signal(barrier, inc=1, device_id=(p, lax.rem(w + k, n)), device_id_type=MESH)
    pl.semaphore_wait(barrier, n - 1)

    def shard(offset):
        return 2 * chip_at(place + offset, chips) + core

    def remote(src, dst, send, recv, to):
        copy = pltpu.make_async_remote_copy(
            src_ref=src, dst_ref=dst, send_sem=send, recv_sem=recv, device_id=(p, to), device_id_type=MESH
        )
        copy.start()
        return copy

    def window(owner, start, size):
        return rows_ref.at[pl.ds(pl.multiple_of(owner * rows + start, 16), size), :]

    sent = []
    cut = rows // 2
    ring = {}

    def pass_on(direction, step, source, owner):
        to = ahead if direction == 0 else behind
        if step < half:
            start, size = 0, rows
        else:
            start, size = (0, cut) if direction == 0 else (cut, rows - cut)
        if source is None:
            src = window(owner, start, size)
        else:
            src = source.at[pl.ds(start, size), :]
        ring[direction, step] = remote(
            src, window(owner, start, size), ring_send.at[direction, step], ring_recv.at[direction, step], to
        )

    pass_on(0, 1, prompt_ref, w)
    pass_on(1, 1, prompt_ref, w)
    sent.append(remote(prompt_ref, window(w, 0, rows), core_send.at[0], core_recv.at[0], partner))
    locals_ = [
        pltpu.make_async_copy(prompt_ref, window(w, 0, rows), local_sem.at[0]),
        pltpu.make_async_copy(
            send_ref.at[w], maps_ref.at[:, pl.ds(pl.multiple_of(w * columns, 128), columns)], local_sem.at[1]
        ),
        pltpu.make_async_copy(send_pair_ref.at[w], pairs_ref.at[w], local_sem.at[2]),
    ]
    for copy in locals_:
        copy.start()
    parts = []
    for k in range(1, n):
        to = lax.rem(w + k, n)
        parts.append(
            remote(
                send_ref.at[to],
                maps_ref.at[:, pl.ds(pl.multiple_of(w * columns, 128), columns)],
                part_send.at[0, k], part_recv.at[0, k], to,
            )
        )
        parts.append(
            remote(send_pair_ref.at[to], pairs_ref.at[w], part_send.at[1, k], part_recv.at[1, k], to)
        )
    slot = 1
    for step in range(1, half + 1):
        from_behind, from_ahead = shard(-step), shard(step)
        ring[0, step].wait_recv()
        if step < half:
            pass_on(0, step + 1, None, from_behind)
        ring[1, step].wait_recv()
        if step < half:
            pass_on(1, step + 1, None, from_ahead)
        arrived = (from_behind, from_ahead) if step < half else (from_behind,)
        for owner in arrived:
            here = window(owner, 0, rows)
            sent.append(remote(here, here, core_send.at[slot], core_recv.at[slot], partner))
            slot += 1
    for copy in ring.values():
        copy.wait_send()
    for copy in sent:
        copy.wait_send()
        copy.wait_recv()
    for copy in parts:
        copy.wait_send()
        copy.wait_recv()
    for copy in locals_:
        copy.wait()


def gather(n, send, send_pair, prompt_rows):
    _, map_rows, columns = send.shape
    rows, width = prompt_rows.shape
    chips = n // 2
    half = chips // 2
    any_spec = pl.BlockSpec(memory_space=pl.ANY)
    return pl.pallas_call(
        functools.partial(gather_kernel, n),
        out_shape=(
            jax.ShapeDtypeStruct((map_rows, n * columns), jnp.bfloat16),
            jax.ShapeDtypeStruct(send_pair.shape, jnp.bfloat16),
            jax.ShapeDtypeStruct((n * rows, width), jnp.bfloat16),
        ),
        in_specs=[any_spec] * 3,
        out_specs=(any_spec,) * 3,
        scratch_shapes=[
            pltpu.SemaphoreType.DMA((3,)),
            pltpu.SemaphoreType.DMA((2, half + 1)),
            pltpu.SemaphoreType.DMA((2, half + 1)),
            pltpu.SemaphoreType.DMA((chips,)),
            pltpu.SemaphoreType.DMA((chips,)),
            pltpu.SemaphoreType.DMA((2, n)),
            pltpu.SemaphoreType.DMA((2, n)),
        ],
        compiler_params=pltpu.CompilerParams(collective_id=0, has_side_effects=True),
    )(send, send_pair, prompt_rows)


def spread_kernel(groups, n, maps_ref, pairs_ref, back_ref, back_pair_ref,
                  local_sem, part_send, part_recv, far_send, far_recv):
    p = lax.axis_index("prompt")
    w = lax.axis_index("wide")
    columns = back_ref.shape[3]

    barrier = pltpu.get_barrier_semaphore()
    for k in range(1, n):
        pl.semaphore_signal(barrier, inc=1, device_id=(p, lax.rem(w + k, n)), device_id_type=MESH)
    for k in range(1, groups):
        pl.semaphore_signal(barrier, inc=1, device_id=(lax.rem(p + k, groups), w), device_id_type=MESH)
    pl.semaphore_wait(barrier, n + groups - 2)

    def remote(src, dst, send, recv, to):
        copy = pltpu.make_async_remote_copy(
            src_ref=src, dst_ref=dst, send_sem=send, recv_sem=recv, device_id=to, device_id_type=MESH
        )
        copy.start()
        return copy

    def mine(to):
        return maps_ref.at[:, pl.ds(pl.multiple_of(to * columns, 128), columns)]

    locals_ = [
        pltpu.make_async_copy(mine(w), back_ref.at[p, w], local_sem.at[0]),
        pltpu.make_async_copy(pairs_ref.at[w], back_pair_ref.at[p, w], local_sem.at[1]),
    ]
    for copy in locals_:
        copy.start()
    parts = []
    for k in range(1, n):
        to = lax.rem(w + k, n)
        parts.append((
            remote(mine(to), back_ref.at[p, w], part_send.at[0, k], part_recv.at[0, k], (p, to)),
            remote(pairs_ref.at[to], back_pair_ref.at[p, w], part_send.at[1, k], part_recv.at[1, k], (p, to)),
        ))
    far = []

    def pass_on(owner, slot, source, source_pair):
        for k in range(1, groups):
            to = (lax.rem(p + k, groups), w)
            far.append(
                remote(source, back_ref.at[p, owner], far_send.at[0, k, slot], far_recv.at[0, k, slot], to)
            )
            far.append(
                remote(source_pair, back_pair_ref.at[p, owner], far_send.at[1, k, slot], far_recv.at[1, k, slot], to)
            )

    pass_on(w, 0, mine(w), pairs_ref.at[w])
    for k in range(1, n):
        owner = lax.rem(w - k + n, n)
        parts[k - 1][0].wait_recv()
        parts[k - 1][1].wait_recv()
        pass_on(owner, k, back_ref.at[p, owner], back_pair_ref.at[p, owner])
    for pair in parts:
        for copy in pair:
            copy.wait_send()
    for copy in far:
        copy.wait_send()
        copy.wait_recv()
    for copy in locals_:
        copy.wait()


def spread(groups, n, maps, pairs):
    map_rows, width = maps.shape
    columns = width // n
    any_spec = pl.BlockSpec(memory_space=pl.ANY)
    return pl.pallas_call(
        functools.partial(spread_kernel, groups, n),
        out_shape=(
            jax.ShapeDtypeStruct((groups, n, map_rows, columns), jnp.bfloat16),
            jax.ShapeDtypeStruct((groups,) + pairs.shape, jnp.bfloat16),
        ),
        in_specs=[any_spec] * 2,
        out_specs=(any_spec,) * 2,
        scratch_shapes=[
            pltpu.SemaphoreType.DMA((2,)),
            pltpu.SemaphoreType.DMA((2, n)),
            pltpu.SemaphoreType.DMA((2, n)),
            pltpu.SemaphoreType.DMA((2, groups, n)),
            pltpu.SemaphoreType.DMA((2, groups, n)),
        ],
        compiler_params=pltpu.CompilerParams(collective_id=1, has_side_effects=True),
    )(maps, pairs)


def block_kernel(end_ref, x_ref, query_ref, own_key_ref, own_value_ref, key_ref, value_ref, maps_ref,
                 pairs_ref, cotangent_ref, context_cotangent_ref, grads_ref, pair_grads_ref,
                 low_t, low, up_out, up_out_t, sums):
    head = pl.program_id(0)
    inverse_root = HEAD_DIM ** (-0.5)
    pair_columns = pairs_ref.shape[2]
    pieces = HEAD_DIM // pair_columns
    prompt_len = key_ref.shape[0]

    @pl.when(head == 0)
    def _():
        x = x_ref[...]
        low_t[...] = dot(x, maps_ref[0:48, :], NT).astype(jnp.bfloat16)
        low[...] = dot(maps_ref[0:48, :], x, NT).astype(jnp.bfloat16)
        up_out_t[...] = (adapter_scale * dot(cotangent_ref[...], maps_ref[80:96, :], NT)).astype(jnp.bfloat16)
        up_out[...] = (adapter_scale * dot(maps_ref[80:96, :], cotangent_ref[...], NT)).astype(jnp.bfloat16)
        sums[...] = jnp.zeros_like(sums)

    columns = pl.ds(pl.multiple_of(head * GROUP_WIDTH, GROUP_WIDTH), GROUP_WIDTH)
    down_out = maps_ref[48:64, columns]
    up_query = maps_ref[64:80, columns]
    up_pair = jnp.concatenate([pairs_ref[head * pieces + i] for i in range(pieces)], axis=1)

    queries = (
        query_ref[...].astype(jnp.float32) + adapter_scale * dot(low_t[:, 0:16], up_query)
    ).astype(jnp.bfloat16)
    own_key = (
        own_key_ref[...].astype(jnp.float32) + adapter_scale * dot(low_t[:, 16:32], up_pair[0:16])
    ).astype(jnp.bfloat16)
    own_value = (
        own_value_ref[...].astype(jnp.float32) + adapter_scale * dot(low_t[:, 32:48], up_pair[16:32])
    ).astype(jnp.bfloat16)
    context_grad = (
        context_cotangent_ref[...].astype(jnp.float32) + dot(up_out_t[...], down_out)
    ).astype(jnp.bfloat16)

    limit = end_ref[0, 0] * BLOCK_TOKENS
    prompt_bias = jnp.where(
        lax.broadcasted_iota(jnp.int32, (1, prompt_len), 1) < limit, 0.0, masked_score
    )
    together = 2
    row = lax.broadcasted_iota(jnp.int32, (together * BLOCK_TOKENS, BLOCK_TOKENS), 0) % BLOCK_TOKENS
    column = lax.broadcasted_iota(jnp.int32, (together * BLOCK_TOKENS, BLOCK_TOKENS), 1)
    own_bias = jnp.where(column <= row, 0.0, masked_score)

    def stack(array, first):
        return jnp.concatenate(
            [array[:, (first + i) * HEAD_DIM:(first + i + 1) * HEAD_DIM] for i in range(together)], axis=0
        )

    def side(array):
        return [array[i * BLOCK_TOKENS:(i + 1) * BLOCK_TOKENS] for i in range(together)]

    keys = key_ref[...]
    values = value_ref[...]
    contexts, query_grads = [], []
    key_grad = jnp.zeros((BLOCK_TOKENS, HEAD_DIM), jnp.float32)
    value_grad = jnp.zeros((BLOCK_TOKENS, HEAD_DIM), jnp.float32)
    for first in range(0, HEAD_GROUP, together):
        q = stack(queries, first)
        g = stack(context_grad, first)
        scores = dot(q, keys, NT) + prompt_bias
        own_scores = dot(q, own_key, NT) + own_bias
        peak = jnp.maximum(
            jnp.max(scores, axis=1, keepdims=True), jnp.max(own_scores, axis=1, keepdims=True)
        )
        exponent = jnp.exp2((scores - peak) * (inverse_root * LOG2E))
        own_exponent = jnp.exp2((own_scores - peak) * (inverse_root * LOG2E))
        total = jnp.sum(exponent, axis=1, keepdims=True) + jnp.sum(own_exponent, axis=1, keepdims=True)
        share = 1.0 / total
        weighted = dot(exponent.astype(jnp.bfloat16), values) + dot(own_exponent.astype(jnp.bfloat16), own_value)
        context = (weighted * share).astype(jnp.bfloat16)
        delta = jnp.sum(g.astype(jnp.float32) * context.astype(jnp.float32), axis=1, keepdims=True)
        score_grad = (exponent * share * (dot(g, values, NT) - delta)).astype(jnp.bfloat16)
        own_attention = own_exponent * share
        own_score_grad = (own_attention * (dot(g, own_value, NT) - delta)).astype(jnp.bfloat16)
        query_grad = ((dot(score_grad, keys) + dot(own_score_grad, own_key)) * inverse_root).astype(jnp.bfloat16)
        key_grad += dot(own_score_grad, q, TN)
        value_grad += dot(own_attention.astype(jnp.bfloat16), g, TN)
        contexts += side(context)
        query_grads += side(query_grad)
    context = jnp.concatenate(contexts, axis=1)
    query_grad = jnp.concatenate(query_grads, axis=1)
    key_grad = (key_grad * inverse_root).astype(jnp.bfloat16)
    value_grad = value_grad.astype(jnp.bfloat16)

    sums[0:16, :] += dot(up_query, query_grad, NT)
    sums[16:32, :] += dot(up_pair[0:16], key_grad, NT)
    sums[32:48, :] += dot(up_pair[16:32], value_grad, NT)
    sums[48:64, :] += dot(down_out, context, NT)
    grads_ref[48:64, columns] = dot(up_out[...], context).astype(jnp.bfloat16)
    grads_ref[64:80, columns] = (adapter_scale * dot(low[0:16, :], query_grad)).astype(jnp.bfloat16)
    pair_grad = jnp.concatenate(
        [dot(low[16:32, :], key_grad), dot(low[32:48, :], value_grad)], axis=0
    ) * adapter_scale
    pair_grad = pair_grad.astype(jnp.bfloat16)
    for i in range(pieces):
        pair_grads_ref[head * pieces + i] = pair_grad[:, i * pair_columns:(i + 1) * pair_columns]

    @pl.when(head == KV_HEADS - 1)
    def _():
        up_low = (adapter_scale * sums[0:48, :]).astype(jnp.bfloat16)
        out_low = sums[48:64, :].astype(jnp.bfloat16)
        grads_ref[0:48, :] = dot(up_low, x_ref[...]).astype(jnp.bfloat16)
        grads_ref[80:96, :] = (adapter_scale * dot(out_low, cotangent_ref[...])).astype(jnp.bfloat16)


def block_gradients(end, x, query, own_pair, prompt_rows, maps, pairs, cotangent, context_cotangent):
    tokens, width = x.shape
    prompt_len = prompt_rows.shape[0]

    def whole(array):
        return pl.BlockSpec(array.shape, lambda k: (0,) * array.ndim)

    return pl.pallas_call(
        block_kernel,
        grid=(KV_HEADS,),
        out_shape=(
            jax.ShapeDtypeStruct(maps.shape, jnp.bfloat16),
            jax.ShapeDtypeStruct(pairs.shape, jnp.bfloat16),
        ),
        in_specs=[
            pl.BlockSpec(memory_space=pltpu.SMEM),
            whole(x),
            pl.BlockSpec((tokens, GROUP_WIDTH), lambda k: (0, k)),
            pl.BlockSpec((tokens, HEAD_DIM), lambda k: (0, k)),
            pl.BlockSpec((tokens, HEAD_DIM), lambda k: (0, KV_HEADS + k)),
            pl.BlockSpec((prompt_len, HEAD_DIM), lambda k: (0, k)),
            pl.BlockSpec((prompt_len, HEAD_DIM), lambda k: (0, KV_HEADS + k)),
            whole(maps),
            whole(pairs),
            whole(cotangent),
            pl.BlockSpec((tokens, GROUP_WIDTH), lambda k: (0, k)),
        ],
        out_specs=(whole(maps), whole(pairs)),
        scratch_shapes=[
            pltpu.VMEM((tokens, 48), jnp.bfloat16),
            pltpu.VMEM((48, tokens), jnp.bfloat16),
            pltpu.VMEM((16, tokens), jnp.bfloat16),
            pltpu.VMEM((tokens, 16), jnp.bfloat16),
            pltpu.VMEM((64, tokens), jnp.float32),
        ],
        compiler_params=pltpu.CompilerParams(vmem_limit_bytes=48 * 1024 * 1024),
    )(end, x, query, own_pair, own_pair, prompt_rows, prompt_rows, maps, pairs, cotangent, context_cotangent)


def total_kernel(groups, n, ids_ref, back_ref, back_pair_ref, down_ref, up_ref, pair_ref):
    down_ref[...] = jnp.zeros_like(down_ref)
    up_ref[...] = jnp.zeros_like(up_ref)
    pair_ref[...] = jnp.zeros_like(pair_ref)
    for group in range(groups):
        def step(source, carry):
            adapter = ids_ref[group, source]
            for part in range(4):
                down_ref[adapter, part] += back_ref[group, source, 16 * part:16 * (part + 1)].astype(jnp.float32)
            for part in range(2):
                up_ref[adapter, part] += back_ref[group, source, 64 + 16 * part:80 + 16 * part].astype(jnp.float32)
                pair_ref[adapter, part] += back_pair_ref[group, source, 16 * part:16 * (part + 1)].astype(jnp.float32)
            return carry

        lax.fori_loop(0, n, step, 0)


def totals(ids, back, back_pair):
    groups, n, _, columns = back.shape
    vmem = pl.BlockSpec(memory_space=pltpu.VMEM)
    return pl.pallas_call(
        functools.partial(total_kernel, groups, n),
        out_shape=(
            jax.ShapeDtypeStruct((ADAPTER_COUNT, 4, RANK, columns), jnp.float32),
            jax.ShapeDtypeStruct((ADAPTER_COUNT, 2, RANK, columns), jnp.float32),
            jax.ShapeDtypeStruct((ADAPTER_COUNT, 2, RANK, back_pair.shape[3]), jnp.float32),
        ),
        in_specs=[pl.BlockSpec(memory_space=pltpu.SMEM), vmem, vmem],
        out_specs=(vmem, vmem, vmem),
        compiler_params=pltpu.CompilerParams(vmem_limit_bytes=48 * 1024 * 1024),
    )(ids, back, back_pair)


def body(
    groups, n,
    candidate_hidden,
    frozen_query,
    candidate_key_value,
    prompt_key_value,
    candidate_adapter,
    prompt_block_end,
    adapter_down,
    adapter_up,
    adapter_up_key_value,
    output_cotangent,
    context_cotangent,
):
    ids = candidate_adapter[0]
    columns = adapter_down.shape[3]
    all_ids = lax.all_gather(ids, "prompt", axis=0)
    send = jnp.concatenate(
        [adapter_down[ids].reshape(n, 4 * RANK, columns), adapter_up[ids].reshape(n, 2 * RANK, columns)], axis=1
    )
    send_pair = adapter_up_key_value[ids].reshape(n, 2 * RANK, adapter_up_key_value.shape[3])
    maps, pairs, prompt_rows = gather(n, send, send_pair, prompt_key_value[0])
    grads, pair_grads = block_gradients(
        prompt_block_end, candidate_hidden[0], frozen_query[0], candidate_key_value[0], prompt_rows,
        maps, pairs, output_cotangent[0], context_cotangent[0],
    )
    back, back_pair = spread(groups, n, grads, pair_grads)
    return totals(all_ids, back, back_pair)


def solution(mesh):
    placed = (
        P("prompt", "wide", None),
        P("prompt", "wide", None),
        P("prompt", "wide", None),
        P("prompt", "wide", None),
        P("prompt", None),
        P("prompt", "wide"),
        P(None, None, None, "wide"),
        P(None, None, None, "wide"),
        P(None, None, None, "wide"),
        P("prompt", "wide", None),
        P("prompt", "wide", None),
    )
    return jax.shard_map(
        functools.partial(body, mesh.shape["prompt"], mesh.shape["wide"]),
        mesh=mesh,
        in_specs=placed,
        out_specs=(
            P(None, None, None, "wide"),
            P(None, None, None, "wide"),
            P(None, None, None, "wide"),
        ),
        check_vma=False,
    )
```

time: 446 us -> 135 us (0.30)
  waiting for transfers between devices: 282 us -> 0 us
  Pallas kernels: 0 us -> 115 us
  local copies, waits for them, and re-layouts: 71.1 us -> 11.6 us
  matrix products: 48.2 us -> 0 us
  starting transfers between devices: 18.6 us -> 0 us
  between operations: 16.8 us -> 1.4 us
    all_gather x4 -> x0, waiting for transfers between devices: 235 us -> none  [the longest x1 72.4 us: body(): lax.all_gather(adapter_down, 'wide', axis=3, tiled=True)]
    pallas_call x0 -> x4, Pallas kernels: none -> 115 us  [the longest x1 49.4 us: gather(): pl.pallas_call(functools.partial(gather_kernel, n), out_shape=(jax.ShapeD...]
    dot_general x24 -> x0, matrix products: 48.2 us -> none  [the longest x1 12.9 us: body(): jnp.einsum('kgbj,jkd->bkgd', score_grad, key_heads, preferred_element_typ...]
    psum x1 -> x0, waiting for transfers between devices: 39.1 us -> none  [body(): lax.psum(owned_a.astype(jnp.bfloat16), 'prompt').astype(jnp.float32)]
    unnamed x61 -> x26, local copies, waits for them, and re-layouts: 35.6 us -> 7.5 us
    all_to_all x3 -> x0, starting transfers between devices: 18.4 us -> none  [the longest x1 6.34 us: body(): lax.all_to_all(key_value_up_gradient.astype(jnp.bfloat16), 'wide', split_...]
    another operation x5 -> x0, local copies, waits for them, and re-layouts: 8.04 us -> none  [the longest x1 3.8 us: body(): jnp.stack([adapter_scale * jnp.einsum('crb,cbd->crd', rank_projection[:,...]
    all_gather x1 -> x0, local copies, waits for them, and re-layouts: 6.4 us -> none  [body(): gathered = lax.all_gather(prompt_key_value, 'wide', axis=1, tiled=True)]
  transfers between devices with their start and end apart: 8 -> 0, of which waited for: 6 -> 0; matrix products, arithmetic and copies ran while one was open for 12% -> 0% of each run, Pallas kernels for 0% -> 0%
where the time goes in v1:
time: 135 us
  Pallas kernels  115 us (85%)
  local copies, waits for them, and re-layouts  11.6 us (9%)
  blocking collectives  4.22 us (3%)
  other arithmetic  2.86 us (2%)
  between operations  1.4 us (1%)
    pallas_call x1, Pallas kernels, gather(): pl.pallas_call(functools.partial(gather_kernel, n), out_shape=(jax.ShapeD...  49.4 us
    pallas_call x1, Pallas kernels, spread(): pl.pallas_call(functools.partial(spread_kernel, groups, n), out_shape=(ja...  38.5 us
    pallas_call x1, Pallas kernels, block_gradients(): pl.pallas_call(block_kernel, grid=(KV_HEADS,), out_shape=(jax.ShapeDtypeS...  24.4 us
    unnamed x26, local copies, waits for them, and re-layouts  7.5 us
    all_gather x1, blocking collectives, body(): all_ids = lax.all_gather(ids, 'prompt', axis=0)  4.22 us

profile of v1, /device:TPU:24, one launch (start us, length us, event | category | flops | bytes accessed | tf_op | source)
XLA Modules:
  0.0 134.8 jit_solution(12926348370475725460)
XLA Ops:
  0.6 0.0 copy-start
  0.6 0.7 fusion
  1.4 0.3 copy-done
  1.7 1.4 %gather_fusion = bf16[16,4,16,256]{3,2,1,0:T(8,128)(2,1)} fusion(bf16[16,4,16,256]{3,2,1,0:T(8,128)(2,1)S(1)} %copy-done, s32[1024]{0:T(1024)S(1)} %pad_clamp_fusion), kind=kCustom, calls=%fused_computation | custom fusion | bytes 1048640 | tf_op jit(solution)/shard_map/gather | solution.py:452
  3.1 1.5 %gather_fusion.1 = bf16[16,2,16,256]{3,2,1,0:T(8,128)(2,1)S(1)} fusion(bf16[16,2,16,256]{3,2,1,0:T(8,128)(2,1)} %param.18, s32[1024]{0:T(1024)S(1)} %pad_clamp_fusion), kind=kCustom, calls=%fused_computation.1 | custom fusion | bytes 524352 | tf_op jit(solution)/shard_map/gather | solution.py:452
  4.6 0.0 copy-start.1
  4.6 0.0 copy-start.3
  4.6 0.0 copy-start.4
  4.6 2.1 %pad_maximum_fusion.send_ref = bf16[16,96,256]{2,1,0:T(8,128)(2,1)} fusion(bf16[16,32,256]{2,1,0:T(8,128)(2,1)S(1)} %bitcast.23, bf16[16,64,256]{2,1,0:T(8,128)(2,1)} %bitcast.21), kind=kLoop, calls=%fused_computation.3 | loop fusion | flops 1572864 | bytes 1572864 | tf_op jit(solution)/shard_map/concatenate | solution.py:451
  6.8 1.2 gather_fusion.2
  8.0 49.4 %shard_map.130 = (bf16[96,4096]{1,0:T(8,128)(2,1)}, bf16[16,32,64]{2,1,0:T(8,128)(2,1)}, bf16[1024,2048]{1,0:T(8,128)(2,1)}) custom-call(bf16[16,96,256]{2,1,0:T(8,128)(2,1)} %pad_maximum_fusion.send_ref, bf16[16,32,64]{2,1,0:T(8,128)(2,1)} %bitcast.24, bf16[64,2048]{1,0:T(8,128)(2,1)} %bitcast.25), custom_call_target="tpu_custom_call" | custom-call | tf_op jit(solution)/shard_map/pallas_call | solution.py:146
  58.1 0.0 copy-start.5
  58.1 1.2 copy-done.5
  59.3 1.1 copy-done.6
  60.5 0.9 copy-done.9
  61.4 24.4 %shard_map.131 = (bf16[96,4096]{1,0:T(8,128)(2,1)S(1)}, bf16[16,32,64]{2,1,0:T(8,128)(2,1)S(1)}) custom-call(s32[1,1]{1,0:T(1,128)S(6)} %copy.14.end_ref, bf16[128,4096]{1,0:T(8,128)(2,1)S(1)} %bitcast.17, bf16[128,4096]{1,0:T(8,128)(2,1)S(1)} %bitcast.18, bf16[128,2048]{1,0:T(8,128)(2,1)S(1)} %bitcast.15, bf16[128,2048]{1,0:T(8,128)(2,1)S(1)} %bitcast.16, ...), custom_call_target="tpu_custom_call" | custom-call | tf_op jit(solution)/shard_map/pallas_call | solution.py:369
  85.8 0.0 copy-start.7
  85.8 0.9 copy-done.7
  86.7 0.7 copy-done.10
  87.4 38.5 %shard_map.132 = (bf16[2,16,96,256]{3,2,1,0:T(8,128)(2,1)}, bf16[2,16,32,64]{3,2,1,0:T(8,128)(2,1)}) custom-call(bf16[96,4096]{1,0:T(8,128)(2,1)} %copy-done.7, bf16[16,32,64]{2,1,0:T(8,128)(2,1)} %copy-done.10), custom_call_target="tpu_custom_call" | custom-call | tf_op jit(solution)/shard_map/pallas_call | solution.py:236
  125.9 4.2 %all-gather = s32[2,1,16]{2,1,0:T(1,128)S(1)} all-gather(s32[1,1,16]{2,1,0:T(1,128)S(1)} %bitcast.26), channel_id=1, replica_groups=mesh['prompt'=2,'wide'=16] {'prompt'}, dimensions={0}, use_global_device_ids=true | all-gather | bytes 192 | tf_op jit(solution)/shard_map/all_gather | solution.py:450
  130.1 1.4 %copy-done.2 = bf16[2,16,96,256]{3,2,1,0:T(8,128)(2,1)S(1)} copy-done((bf16[2,16,96,256]{3,2,1,0:T(8,128)(2,1)S(1)}, bf16[2,16,96,256]{3,2,1,0:T(8,128)(2,1)}, u32[]{:S(2)}) %copy-start.2) | copy-done | bytes 1572888
  131.5 0.9 copy-done.8
  132.4 2.4 %shard_map.133 = (f32[16,4,16,256]{3,2,1,0:T(8,128)}, f32[16,2,16,256]{3,2,1,0:T(8,128)}, f32[16,2,16,64]{3,2,1,0:T(8,128)}) custom-call(s32[2,16]{1,0:T(2,128)S(1)} %bitcast.20, bf16[2,16,96,256]{3,2,1,0:T(8,128)(2,1)S(1)} %copy-done.2, bf16[2,16,32,64]{3,2,1,0:T(8,128)(2,1)S(1)} %copy-done.8), custom_call_target="tpu_custom_call" | custom-call | tf_op jit(solution)/shard_map/pallas_call | solution.py:421
  (13 shorter events, 0.0 us)
Async XLA Ops:
  0.6 1.1 copy-start
  1.7 5.1 %copy-start.11 = (bf16[16,2,16,64]{3,2,1,0:T(8,128)(2,1)S(1)}, bf16[16,2,16,64]{3,2,1,0:T(8,128)(2,1)}, u32[]{:S(2)}) copy-start(bf16[16,2,16,64]{3,2,1,0:T(8,128)(2,1)} %param.19) | copy-start | bytes 196612
  4.6 53.5 %copy-start.1 = (bf16[1,128,2048]{2,1,0:T(8,128)(2,1)S(1)}, bf16[1,128,2048]{2,1,0:T(8,128)(2,1)}, u32[]{:S(2)}) copy-start(bf16[1,128,2048]{2,1,0:T(8,128)(2,1)} %param.13) | copy-start | bytes 1572868
  4.6 53.5 %copy-start.3 = (bf16[1,128,4096]{2,1,0:T(8,128)(2,1)S(1)}, bf16[1,128,4096]{2,1,0:T(8,128)(2,1)}, u32[]{:S(2)}) copy-start(bf16[1,128,4096]{2,1,0:T(8,128)(2,1)} %param.11) | copy-start | bytes 3145732
  4.6 53.5 %copy-start.4 = (bf16[1,128,4096]{2,1,0:T(8,128)(2,1)S(1)}, bf16[1,128,4096]{2,1,0:T(8,128)(2,1)}, u32[]{:S(2)}) copy-start(bf16[1,128,4096]{2,1,0:T(8,128)(2,1)} %param.12) | copy-start | bytes 3145732
  58.1 1.2 copy-start.5
  59.3 1.1 copy-start.6
  60.5 0.9 copy-start.9
  61.4 64.5 %copy-start.12 = (s32[1,16]{1,0:T(1,128)S(1)}, s32[1,16]{1,0:T(1,128)}, u32[]{:S(2)}) copy-start(s32[1,16]{1,0:T(1,128)} %param.15) | copy-start | bytes 196
  85.8 0.9 copy-start.7
  86.7 0.7 copy-start.10
  130.1 1.4 %copy-start.2 = (bf16[2,16,96,256]{3,2,1,0:T(8,128)(2,1)S(1)}, bf16[2,16,96,256]{3,2,1,0:T(8,128)(2,1)}, u32[]{:S(2)}) copy-start(bf16[2,16,96,256]{3,2,1,0:T(8,128)(2,1)} %get-tuple-element.15.back_ref) | copy-start | bytes 4718596
  131.5 0.9 copy-start.8

commit v2 on v1

v2 whole, which is shorter than its diff:
```python
import functools

import jax
import jax.numpy as jnp
from jax import lax
from jax.experimental import pallas as pl
from jax.experimental.pallas import tpu as pltpu
from jax.sharding import PartitionSpec as P

HEADS = 32
KV_HEADS = 8
HEAD_DIM = 128
ADAPTER_COUNT = 16
BLOCK_TOKENS = 128
RANK = 16
HEAD_GROUP = HEADS // KV_HEADS
GROUP_WIDTH = HEAD_GROUP * HEAD_DIM
MESH = pl.DeviceIdType.MESH

adapter_scale = 2.0
masked_score = -1e30
LOG2E = 1.4426950408889634


def dot(a, b, contract=((1,), (0,))):
    return lax.dot_general(a, b, (contract, ((), ())), preferred_element_type=jnp.float32)


NT = ((1,), (1,))
TN = ((0,), (0,))


def chip_at(place, chips):
    place = lax.rem(place + chips, chips)
    return jnp.where(place < chips // 2, 2 * place, 2 * (chips - 1 - place) + 1)


def spread_kernel(groups, n, maps_ref, pairs_ref, ids_ref, back_ref, back_pair_ref, all_ids_ref,
                  local_sem, part_send, part_recv, far_send, far_recv, ids_send, ids_recv):
    p = lax.axis_index("prompt")
    w = lax.axis_index("wide")
    columns = back_ref.shape[3]

    barrier = pltpu.get_barrier_semaphore()
    for k in range(1, n):
        pl.semaphore_signal(barrier, inc=1, device_id=(p, lax.rem(w + k, n)), device_id_type=MESH)
    for k in range(1, groups):
        pl.semaphore_signal(barrier, inc=1, device_id=(lax.rem(p + k, groups), w), device_id_type=MESH)
    pl.semaphore_wait(barrier, n + groups - 2)

    def remote(src, dst, send, recv, to):
        copy = pltpu.make_async_remote_copy(
            src_ref=src, dst_ref=dst, send_sem=send, recv_sem=recv, device_id=to, device_id_type=MESH
        )
        copy.start()
        return copy

    def mine(to):
        return maps_ref.at[:, pl.ds(pl.multiple_of(to * columns, 128), columns)]

    locals_ = [
        pltpu.make_async_copy(mine(w), back_ref.at[p, w], local_sem.at[0]),
        pltpu.make_async_copy(pairs_ref.at[w], back_pair_ref.at[p, w], local_sem.at[1]),
        pltpu.make_async_copy(ids_ref, all_ids_ref.at[p], local_sem.at[2]),
    ]
    for copy in locals_:
        copy.start()
    parts = []
    for k in range(1, n):
        to = lax.rem(w + k, n)
        parts.append((
            remote(mine(to), back_ref.at[p, w], part_send.at[0, k], part_recv.at[0, k], (p, to)),
            remote(pairs_ref.at[to], back_pair_ref.at[p, w], part_send.at[1, k], part_recv.at[1, k], (p, to)),
        ))
    far = [
        remote(ids_ref, all_ids_ref.at[p], ids_send.at[k], ids_recv.at[k], (lax.rem(p + k, groups), w))
        for k in range(1, groups)
    ]

    def pass_on(owner, slot, source, source_pair):
        for k in range(1, groups):
            to = (lax.rem(p + k, groups), w)
            far.append(
                remote(source, back_ref.at[p, owner], far_send.at[0, k, slot], far_recv.at[0, k, slot], to)
            )
            far.append(
                remote(source_pair, back_pair_ref.at[p, owner], far_send.at[1, k, slot], far_recv.at[1, k, slot], to)
            )

    pass_on(w, 0, mine(w), pairs_ref.at[w])
    for k in range(1, n):
        owner = lax.rem(w - k + n, n)
        parts[k - 1][0].wait_recv()
        parts[k - 1][1].wait_recv()
        pass_on(owner, k, back_ref.at[p, owner], back_pair_ref.at[p, owner])
    for pair in parts:
        for copy in pair:
            copy.wait_send()
    for copy in far:
        copy.wait_send()
        copy.wait_recv()
    for copy in locals_:
        copy.wait()


def spread(groups, n, maps, pairs, ids):
    map_rows, width = maps.shape
    columns = width // n
    any_spec = pl.BlockSpec(memory_space=pl.ANY)
    return pl.pallas_call(
        functools.partial(spread_kernel, groups, n),
        out_shape=(
            jax.ShapeDtypeStruct((groups, n, map_rows, columns), jnp.bfloat16),
            jax.ShapeDtypeStruct((groups,) + pairs.shape, jnp.bfloat16),
            jax.ShapeDtypeStruct((groups,) + ids.shape, jnp.int32),
        ),
        in_specs=[any_spec] * 3,
        out_specs=(any_spec,) * 3,
        scratch_shapes=[
            pltpu.SemaphoreType.DMA((3,)),
            pltpu.SemaphoreType.DMA((2, n)),
            pltpu.SemaphoreType.DMA((2, n)),
            pltpu.SemaphoreType.DMA((2, groups, n)),
            pltpu.SemaphoreType.DMA((2, groups, n)),
            pltpu.SemaphoreType.DMA((groups,)),
            pltpu.SemaphoreType.DMA((groups,)),
        ],
        compiler_params=pltpu.CompilerParams(collective_id=1, has_side_effects=True),
    )(maps, pairs, ids)


PIECES = 4
PIECE_HEADS = KV_HEADS // PIECES
PIECE_WIDTH = PIECE_HEADS * HEAD_DIM


def block_kernel(n, end_ref, x_ref, query_ref, own_ref, cotangent_ref, context_cotangent_ref,
                 send_down_ref, send_up_ref, send_pair_ref, prompt_ref, grads_ref, pair_grads_ref,
                 maps_ref, pairs_ref, rows_ref, low_t, low, up_out, up_out_t, sums,
                 local_sem, own_sem, ring_send, ring_recv, core_send, core_recv, part_send, part_recv):
    p = lax.axis_index("prompt")
    w = lax.axis_index("wide")
    chips = n // 2
    half = chips // 2
    core = lax.rem(w, 2)
    chip = w // 2
    place = jnp.where(lax.rem(chip, 2) == 0, chip // 2, chips - 1 - chip // 2)
    rows = prompt_ref.shape[1]
    cut = rows // 2
    map_columns = send_down_ref.shape[2]
    partner = w + 1 - 2 * core
    ahead = 2 * chip_at(place + 1, chips) + core
    behind = 2 * chip_at(place - 1, chips) + core

    barrier = pltpu.get_barrier_semaphore()
    for k in range(1, n):
        pl.semaphore_signal(barrier, inc=1, device_id=(p, lax.rem(w + k, n)), device_id_type=MESH)
    pl.semaphore_wait(barrier, n - 1)

    def shard(offset):
        return 2 * chip_at(place + offset, chips) + core

    def remote(src, dst, send, recv, to):
        return pltpu.make_async_remote_copy(
            src_ref=src, dst_ref=dst, send_sem=send, recv_sem=recv, device_id=(p, to), device_id_type=MESH
        )

    def window(piece, owner, start, size):
        return rows_ref.at[piece, pl.ds(pl.multiple_of(owner * rows + start, 16), size), :]

    def ring(piece, direction, step):
        owner = shard(1 - step) if direction == 0 else shard(step - 1)
        if step < half:
            start, size = 0, rows
        else:
            start, size = (0, cut) if direction == 0 else (cut, rows - cut)
        if step == 1:
            src = prompt_ref.at[piece, pl.ds(start, size), :]
        else:
            src = window(piece, owner, start, size)
        return remote(
            src, window(piece, owner, start, size), ring_send.at[piece, direction, step],
            ring_recv.at[piece, direction, step], ahead if direction == 0 else behind,
        )

    def across(piece, slot):
        if slot == 0:
            src, owner = prompt_ref.at[piece], w
        else:
            step = (slot + 1) // 2
            owner = shard(-step) if slot % 2 == 1 else shard(step)
            src = window(piece, owner, 0, rows)
        return remote(
            src, window(piece, owner, 0, rows), core_send.at[piece, slot], core_recv.at[piece, slot], partner
        )

    def own_copy(piece):
        return pltpu.make_async_copy(prompt_ref.at[piece], window(piece, w, 0, rows), own_sem.at[piece])

    def begin(piece):
        ring(piece, 0, 1).start()
        ring(piece, 1, 1).start()
        across(piece, 0).start()
        own_copy(piece).start()

    def hop(piece, step):
        for direction in range(2):
            ring(piece, direction, step).wait_recv()
            if step < half:
                ring(piece, direction, step + 1).start()
        across(piece, 2 * step - 1).start()
        if step < half:
            across(piece, 2 * step).start()

    part_columns = pl.ds(pl.multiple_of(w * map_columns, 128), map_columns)
    down_here = maps_ref.at[0:64, part_columns]
    up_here = maps_ref.at[64:96, part_columns]
    pair_here = pairs_ref.at[w]
    locals_ = [
        pltpu.make_async_copy(send_down_ref.at[w], down_here, local_sem.at[0]),
        pltpu.make_async_copy(send_up_ref.at[w], up_here, local_sem.at[1]),
        pltpu.make_async_copy(send_pair_ref.at[w], pair_here, local_sem.at[2]),
    ]
    for copy in locals_:
        copy.start()
    parts = []
    for k in range(1, n):
        to = lax.rem(w + k, n)
        for i, (src, dst) in enumerate((
            (send_down_ref.at[to], down_here), (send_up_ref.at[to], up_here), (send_pair_ref.at[to], pair_here)
        )):
            copy = remote(src, dst, part_send.at[i, k], part_recv.at[i, k], to)
            copy.start()
            parts.append(copy)
    begin(0)
    for step in range(1, half + 1):
        hop(0, step)
    begin(1)
    for copy in locals_:
        copy.wait()
    for copy in parts:
        copy.wait_recv()

    inverse_root = HEAD_DIM ** (-0.5)
    pair_columns = pairs_ref.shape[2]
    lanes = HEAD_DIM // pair_columns
    prompt_len = rows_ref.shape[1]

    x = x_ref[...]
    low_t[...] = dot(x, maps_ref[0:48, :], NT).astype(jnp.bfloat16)
    low[...] = dot(maps_ref[0:48, :], x, NT).astype(jnp.bfloat16)
    up_out_t[...] = (adapter_scale * dot(cotangent_ref[...], maps_ref[80:96, :], NT)).astype(jnp.bfloat16)
    up_out[...] = (adapter_scale * dot(maps_ref[80:96, :], cotangent_ref[...], NT)).astype(jnp.bfloat16)
    sums[...] = jnp.zeros_like(sums)

    limit = end_ref[0, 0] * BLOCK_TOKENS

    def one_head(head, carry):
        piece = head // PIECE_HEADS
        inner = lax.rem(head, PIECE_HEADS)

        @pl.when(inner == 0)
        def _():
            own_copy(piece).wait()
            for slot in range(chips):
                across(piece, slot).wait_recv()

        columns = pl.ds(pl.multiple_of(head * GROUP_WIDTH, GROUP_WIDTH), GROUP_WIDTH)
        key_columns = pl.ds(pl.multiple_of(head * HEAD_DIM, HEAD_DIM), HEAD_DIM)
        value_columns = pl.ds(pl.multiple_of((KV_HEADS + head) * HEAD_DIM, HEAD_DIM), HEAD_DIM)
        down_out = maps_ref[48:64, columns]
        up_query = maps_ref[64:80, columns]
        up_pair = jnp.concatenate([pairs_ref[head * lanes + i] for i in range(lanes)], axis=1)

        queries = (
            query_ref[:, columns].astype(jnp.float32) + adapter_scale * dot(low_t[:, 0:16], up_query)
        ).astype(jnp.bfloat16)
        own_key = (
            own_ref[:, key_columns].astype(jnp.float32) + adapter_scale * dot(low_t[:, 16:32], up_pair[0:16])
        ).astype(jnp.bfloat16)
        own_value = (
            own_ref[:, value_columns].astype(jnp.float32) + adapter_scale * dot(low_t[:, 32:48], up_pair[16:32])
        ).astype(jnp.bfloat16)
        context_grad = (
            context_cotangent_ref[:, columns].astype(jnp.float32) + dot(up_out_t[...], down_out)
        ).astype(jnp.bfloat16)
        keys = rows_ref[piece, :, pl.ds(pl.multiple_of(inner * HEAD_DIM, HEAD_DIM), HEAD_DIM)]
        values = rows_ref[piece, :, pl.ds(pl.multiple_of(PIECE_WIDTH + inner * HEAD_DIM, HEAD_DIM), HEAD_DIM)]

        prompt_bias = jnp.where(
            lax.broadcasted_iota(jnp.int32, (1, prompt_len), 1) < limit, 0.0, masked_score
        )
        together = 2
        row = lax.broadcasted_iota(jnp.int32, (together * BLOCK_TOKENS, BLOCK_TOKENS), 0) % BLOCK_TOKENS
        column = lax.broadcasted_iota(jnp.int32, (together * BLOCK_TOKENS, BLOCK_TOKENS), 1)
        own_bias = jnp.where(column <= row, 0.0, masked_score)

        def stack(array, first):
            return jnp.concatenate(
                [array[:, (first + i) * HEAD_DIM:(first + i + 1) * HEAD_DIM] for i in range(together)], axis=0
            )

        def side(array):
            return [array[i * BLOCK_TOKENS:(i + 1) * BLOCK_TOKENS] for i in range(together)]

        contexts, query_grads = [], []
        key_grad = jnp.zeros((BLOCK_TOKENS, HEAD_DIM), jnp.float32)
        value_grad = jnp.zeros((BLOCK_TOKENS, HEAD_DIM), jnp.float32)
        for first in range(0, HEAD_GROUP, together):
            q = stack(queries, first)
            g = stack(context_grad, first)
            scores = dot(q, keys, NT) + prompt_bias
            own_scores = dot(q, own_key, NT) + own_bias
            peak = jnp.maximum(
                jnp.max(scores, axis=1, keepdims=True), jnp.max(own_scores, axis=1, keepdims=True)
            )
            exponent = jnp.exp2((scores - peak) * (inverse_root * LOG2E))
            own_exponent = jnp.exp2((own_scores - peak) * (inverse_root * LOG2E))
            total = jnp.sum(exponent, axis=1, keepdims=True) + jnp.sum(own_exponent, axis=1, keepdims=True)
            share = 1.0 / total
            weighted = dot(exponent.astype(jnp.bfloat16), values) + dot(own_exponent.astype(jnp.bfloat16), own_value)
            context = (weighted * share).astype(jnp.bfloat16)
            delta = jnp.sum(g.astype(jnp.float32) * context.astype(jnp.float32), axis=1, keepdims=True)
            score_grad = (exponent * share * (dot(g, values, NT) - delta)).astype(jnp.bfloat16)
            own_attention = own_exponent * share
            own_score_grad = (own_attention * (dot(g, own_value, NT) - delta)).astype(jnp.bfloat16)
            query_grad = ((dot(score_grad, keys) + dot(own_score_grad, own_key)) * inverse_root).astype(jnp.bfloat16)
            key_grad += dot(own_score_grad, q, TN)
            value_grad += dot(own_attention.astype(jnp.bfloat16), g, TN)
            contexts += side(context)
            query_grads += side(query_grad)
        context = jnp.concatenate(contexts, axis=1)
        query_grad = jnp.concatenate(query_grads, axis=1)
        key_grad = (key_grad * inverse_root).astype(jnp.bfloat16)
        value_grad = value_grad.astype(jnp.bfloat16)

        sums[0:16, :] += dot(up_query, query_grad, NT)
        sums[16:32, :] += dot(up_pair[0:16], key_grad, NT)
        sums[32:48, :] += dot(up_pair[16:32], value_grad, NT)
        sums[48:64, :] += dot(down_out, context, NT)
        grads_ref[48:64, columns] = dot(up_out[...], context).astype(jnp.bfloat16)
        grads_ref[64:80, columns] = (adapter_scale * dot(low[0:16, :], query_grad)).astype(jnp.bfloat16)
        pair_grad = jnp.concatenate(
            [dot(low[16:32, :], key_grad), dot(low[32:48, :], value_grad)], axis=0
        ) * adapter_scale
        pair_grad = pair_grad.astype(jnp.bfloat16)
        for i in range(lanes):
            pair_grads_ref[head * lanes + i] = pair_grad[:, i * pair_columns:(i + 1) * pair_columns]


        following = piece + 1
        for turn in range(PIECE_HEADS):
            @pl.when((inner == turn) & (following < PIECES))
            def _():
                for step in range(1 + turn * half // PIECE_HEADS, 1 + (turn + 1) * half // PIECE_HEADS):
                    hop(following, step)

        @pl.when((inner == PIECE_HEADS - 1) & (following + 1 < PIECES))
        def _():
            begin(following + 1)

        return carry

    lax.fori_loop(0, KV_HEADS, one_head, 0)

    up_low = (adapter_scale * sums[0:48, :]).astype(jnp.bfloat16)
    out_low = sums[48:64, :].astype(jnp.bfloat16)
    grads_ref[0:48, :] = dot(up_low, x_ref[...]).astype(jnp.bfloat16)
    grads_ref[80:96, :] = (adapter_scale * dot(out_low, cotangent_ref[...])).astype(jnp.bfloat16)

    for copy in parts:
        copy.wait_send()
    for piece in range(PIECES):
        for step in range(1, half + 1):
            for direction in range(2):
                ring(piece, direction, step).wait_send()
        for slot in range(chips):
            across(piece, slot).wait_send()


def block_gradients(n, end, x, query, own_pair, cotangent, context_cotangent, send_down, send_up, send_pair, prompt):
    tokens, width = x.shape
    map_rows = send_down.shape[1] + send_up.shape[1]
    chips = n // 2
    steps = chips // 2 + 1
    any_spec = pl.BlockSpec(memory_space=pl.ANY)
    vmem = pl.BlockSpec(memory_space=pltpu.VMEM)
    return pl.pallas_call(
        functools.partial(block_kernel, n),
        out_shape=(
            jax.ShapeDtypeStruct((map_rows, width), jnp.bfloat16),
            jax.ShapeDtypeStruct(send_pair.shape, jnp.bfloat16),
        ),
        in_specs=[pl.BlockSpec(memory_space=pltpu.SMEM)] + [vmem] * 5 + [any_spec] * 4,
        out_specs=(vmem, vmem),
        scratch_shapes=[
            pltpu.VMEM((map_rows, width), jnp.bfloat16),
            pltpu.VMEM(send_pair.shape, jnp.bfloat16),
            pltpu.VMEM((PIECES, n * prompt.shape[1], prompt.shape[2]), jnp.bfloat16),
            pltpu.VMEM((tokens, 48), jnp.bfloat16),
            pltpu.VMEM((48, tokens), jnp.bfloat16),
            pltpu.VMEM((16, tokens), jnp.bfloat16),
            pltpu.VMEM((tokens, 16), jnp.bfloat16),
            pltpu.VMEM((64, tokens), jnp.float32),
            pltpu.SemaphoreType.DMA((3,)),
            pltpu.SemaphoreType.DMA((PIECES,)),
            pltpu.SemaphoreType.DMA((PIECES, 2, steps)),
            pltpu.SemaphoreType.DMA((PIECES, 2, steps)),
            pltpu.SemaphoreType.DMA((PIECES, chips)),
            pltpu.SemaphoreType.DMA((PIECES, chips)),
            pltpu.SemaphoreType.DMA((3, n)),
            pltpu.SemaphoreType.DMA((3, n)),
        ],
        compiler_params=pltpu.CompilerParams(
            collective_id=0, has_side_effects=True, vmem_limit_bytes=48 * 1024 * 1024
        ),
    )(end, x, query, own_pair, cotangent, context_cotangent, send_down, send_up, send_pair, prompt)


def total_kernel(groups, n, ids_ref, back_ref, back_pair_ref, down_ref, up_ref, pair_ref):
    down_ref[...] = jnp.zeros_like(down_ref)
    up_ref[...] = jnp.zeros_like(up_ref)
    pair_ref[...] = jnp.zeros_like(pair_ref)
    for group in range(groups):
        def step(source, carry):
            adapter = ids_ref[group, 0, source]
            for part in range(4):
                down_ref[adapter, part] += back_ref[group, source, 16 * part:16 * (part + 1)].astype(jnp.float32)
            for part in range(2):
                up_ref[adapter, part] += back_ref[group, source, 64 + 16 * part:80 + 16 * part].astype(jnp.float32)
                pair_ref[adapter, part] += back_pair_ref[group, source, 16 * part:16 * (part + 1)].astype(jnp.float32)
            return carry

        lax.fori_loop(0, n, step, 0)


def totals(ids, back, back_pair):
    groups, n, _, columns = back.shape
    vmem = pl.BlockSpec(memory_space=pltpu.VMEM)
    return pl.pallas_call(
        functools.partial(total_kernel, groups, n),
        out_shape=(
            jax.ShapeDtypeStruct((ADAPTER_COUNT, 4, RANK, columns), jnp.float32),
            jax.ShapeDtypeStruct((ADAPTER_COUNT, 2, RANK, columns), jnp.float32),
            jax.ShapeDtypeStruct((ADAPTER_COUNT, 2, RANK, back_pair.shape[3]), jnp.float32),
        ),
        in_specs=[pl.BlockSpec(memory_space=pltpu.SMEM), vmem, vmem],
        out_specs=(vmem, vmem, vmem),
        compiler_params=pltpu.CompilerParams(vmem_limit_bytes=48 * 1024 * 1024),
    )(ids, back, back_pair)


def body(
    groups, n,
    candidate_hidden,
    frozen_query,
    candidate_key_value,
    prompt_key_value,
    candidate_adapter,
    prompt_block_end,
    adapter_down,
    adapter_up,
    adapter_up_key_value,
    output_cotangent,
    context_cotangent,
):
    ids = candidate_adapter[0]
    columns = adapter_down.shape[3]
    send_down = adapter_down[ids].reshape(n, 4 * RANK, columns)
    send_up = adapter_up[ids].reshape(n, 2 * RANK, columns)
    send_pair = adapter_up_key_value[ids].reshape(n, 2 * RANK, adapter_up_key_value.shape[3])
    rows = prompt_key_value.shape[1]
    prompt = jnp.transpose(
        prompt_key_value[0].reshape(rows, 2, PIECES, PIECE_WIDTH), (2, 0, 1, 3)
    ).reshape(PIECES, rows, 2 * PIECE_WIDTH)
    grads, pair_grads = block_gradients(
        n, prompt_block_end, candidate_hidden[0], frozen_query[0], candidate_key_value[0],
        output_cotangent[0], context_cotangent[0], send_down, send_up, send_pair, prompt,
    )
    back, back_pair, all_ids = spread(groups, n, grads, pair_grads, candidate_adapter)
    return totals(all_ids, back, back_pair)


def solution(mesh):
    placed = (
        P("prompt", "wide", None),
        P("prompt", "wide", None),
        P("prompt", "wide", None),
        P("prompt", "wide", None),
        P("prompt", None),
        P("prompt", "wide"),
        P(None, None, None, "wide"),
        P(None, None, None, "wide"),
        P(None, None, None, "wide"),
        P("prompt", "wide", None),
        P("prompt", "wide", None),
    )
    return jax.shard_map(
        functools.partial(body, mesh.shape["prompt"], mesh.shape["wide"]),
        mesh=mesh,
        in_specs=placed,
        out_specs=(
            P(None, None, None, "wide"),
            P(None, None, None, "wide"),
            P(None, None, None, "wide"),
        ),
        check_vma=False,
    )
```

time: 135 us -> 143 us (1.059)
  Pallas kernels: 115 us -> 128 us
  blocking collectives: 4.22 us -> 0 us
  other arithmetic: 2.86 us -> 0.67 us
    pallas_call x2 -> x1, Pallas kernels: 73.9 us -> 86.1 us  [block_gradients(): pl.pallas_call(functools.partial(block_kernel, n), out_shape=(jax.ShapeDt...]
    all_gather x1 -> x0, blocking collectives: 4.22 us -> none  [body(): all_ids = lax.all_gather(ids, 'prompt', axis=0)]
    concatenate x1 -> x0, other arithmetic: 2.13 us -> none  [body(): jnp.concatenate([adapter_down[ids].reshape(n, 4 * RANK, columns), adapter...]
    unnamed x26 -> x20, local copies, waits for them, and re-layouts: 7.5 us -> 7 us
where the time goes in v2:
time: 143 us; the launch traced here: 142 us
  Pallas kernels  128 us (90%)
  local copies, waits for them, and re-layouts  12.2 us (9%)
  between operations  1.47 us (1%)
    pallas_call x1, Pallas kernels, block_gradients(): pl.pallas_call(functools.partial(block_kernel, n), out_shape=(jax.ShapeDt...  86.1 us
    pallas_call x1, Pallas kernels, spread(): pl.pallas_call(functools.partial(spread_kernel, groups, n), out_shape=(ja...  39.3 us
    unnamed x20, local copies, waits for them, and re-layouts  7 us

profile of v2, /device:TPU:24, one launch (start us, length us, event | category | flops | bytes accessed | tf_op | source)
XLA Modules:
  0.0 142.1 jit_solution(7135773031018861818)
XLA Ops:
  0.6 0.0 copy-start
  1.3 0.7 fusion
  2.0 1.5 %gather_fusion.2 = bf16[16,2,16,64]{3,2,1,0:T(8,128)(2,1)S(1)} fusion(bf16[16,2,16,64]{3,2,1,0:T(8,128)(2,1)} %param.19, s32[1024]{0:T(1024)S(1)} %pad_clamp_fusion), kind=kCustom, calls=%fused_computation.2 | custom fusion | bytes 131136 | tf_op jit(solution)/shard_map/gather | solution.py:471
  3.5 0.0 copy-start.2
  3.5 0.0 copy-start.6
  3.5 1.6 %gather_fusion.1 = bf16[16,2,16,256]{3,2,1,0:T(8,128)(2,1)S(1)} fusion(bf16[16,2,16,256]{3,2,1,0:T(8,128)(2,1)} %param.18, s32[1024]{0:T(1024)S(1)} %pad_clamp_fusion), kind=kCustom, calls=%fused_computation.1 | custom fusion | bytes 524352 | tf_op jit(solution)/shard_map/gather | solution.py:470
  5.2 1.1 reshape_squeeze.3
  6.3 0.2 copy.16
  6.5 0.2 reshape.49.prompt_ref
  6.7 0.0 copy-done
  6.7 0.6 gather_fusion
  7.3 0.0 copy-start.3
  7.3 1.2 copy-done.3
  8.5 1.2 copy-done.4
  9.8 86.1 %shard_map.130 = (bf16[96,4096]{1,0:T(8,128)(2,1)S(1)}, bf16[16,32,64]{2,1,0:T(8,128)(2,1)S(1)}) custom-call(s32[1,1]{1,0:T(1,128)S(6)} %copy.17.end_ref, bf16[128,4096]{1,0:T(8,128)(2,1)S(1)} %bitcast.17, bf16[128,4096]{1,0:T(8,128)(2,1)S(1)} %bitcast.18, bf16[128,2048]{1,0:T(8,128)(2,1)S(1)} %bitcast.20, bf16[128,4096]{1,0:T(8,128)(2,1)S(1)} %bitcast.19, ...), custom_call_target="tpu_custom_call" | custom-call | tf_op jit(solution)/shard_map/pallas_call | solution.py:388
  95.9 0.0 copy-start.5
  95.9 0.9 copy-done.5
  96.8 0.7 copy-done.8
  97.4 39.3 %shard_map.131 = (bf16[2,16,96,256]{3,2,1,0:T(8,128)(2,1)}, bf16[2,16,32,64]{3,2,1,0:T(8,128)(2,1)}, s32[2,1,16]{2,1,0:T(1,128)}) custom-call(bf16[96,4096]{1,0:T(8,128)(2,1)} %copy-done.5, bf16[16,32,64]{2,1,0:T(8,128)(2,1)} %copy-done.8, s32[1,16]{1,0:T(1,128)} %ids_ref.1), custom_call_target="tpu_custom_call" | custom-call | tf_op jit(solution)/shard_map/pallas_call | solution.py:110
  136.7 0.0 copy-start.1
  136.7 1.4 copy-done.1
  138.1 0.9 copy-done.7
  139.1 0.7 copy-done.9
  139.8 2.4 %shard_map.132 = (f32[16,4,16,256]{3,2,1,0:T(8,128)}, f32[16,2,16,256]{3,2,1,0:T(8,128)}, f32[16,2,16,64]{3,2,1,0:T(8,128)}) custom-call(s32[2,1,16]{2,1,0:T(1,128)S(1)} %copy-done.9, bf16[2,16,96,256]{3,2,1,0:T(8,128)(2,1)S(1)} %copy-done.1, bf16[2,16,32,64]{3,2,1,0:T(8,128)(2,1)S(1)} %copy-done.7), custom_call_target="tpu_custom_call" | custom-call | tf_op jit(solution)/shard_map/pallas_call | solution.py:440
  (7 shorter events, 0.0 us)
Async XLA Ops:
  0.6 6.1 %copy-start = (bf16[16,4,16,256]{3,2,1,0:T(8,128)(2,1)S(1)}, bf16[16,4,16,256]{3,2,1,0:T(8,128)(2,1)}, u32[]{:S(2)}) copy-start(bf16[16,4,16,256]{3,2,1,0:T(8,128)(2,1)} %param.17) | copy-start | bytes 1572868
  3.5 3.8 %copy-start.2 = (bf16[1,128,4096]{2,1,0:T(8,128)(2,1)S(1)}, bf16[1,128,4096]{2,1,0:T(8,128)(2,1)}, u32[]{:S(2)}) copy-start(bf16[1,128,4096]{2,1,0:T(8,128)(2,1)} %param.11) | copy-start | bytes 3145732
  3.5 3.8 %copy-start.6 = (bf16[1,128,2048]{2,1,0:T(8,128)(2,1)S(1)}, bf16[1,128,2048]{2,1,0:T(8,128)(2,1)}, u32[]{:S(2)}) copy-start(bf16[1,128,2048]{2,1,0:T(8,128)(2,1)} %param.13) | copy-start | bytes 1572868
  7.3 1.2 copy-start.3
  8.5 1.2 copy-start.4
  95.9 0.9 copy-start.5
  96.8 0.7 copy-start.8
  136.7 1.4 copy-start.1
  138.1 0.9 copy-start.7
  139.1 0.7 copy-start.9

commit v3 on v2

--- a/solution.py
+++ b/solution.py
@@ -35,109 +35,20 @@
     return jnp.where(place < chips // 2, 2 * place, 2 * (chips - 1 - place) + 1)
 
 
-def spread_kernel(groups, n, maps_ref, pairs_ref, ids_ref, back_ref, back_pair_ref, all_ids_ref,
-                  local_sem, part_send, part_recv, far_send, far_recv, ids_send, ids_recv):
-    p = lax.axis_index("prompt")
-    w = lax.axis_index("wide")
-    columns = back_ref.shape[3]
-
-    barrier = pltpu.get_barrier_semaphore()
-    for k in range(1, n):
-        pl.semaphore_signal(barrier, inc=1, device_id=(p, lax.rem(w + k, n)), device_id_type=MESH)
-    for k in range(1, groups):
-        pl.semaphore_signal(barrier, inc=1, device_id=(lax.rem(p + k, groups), w), device_id_type=MESH)
-    pl.semaphore_wait(barrier, n + groups - 2)
-
-    def remote(src, dst, send, recv, to):
-        copy = pltpu.make_async_remote_copy(
-            src_ref=src, dst_ref=dst, send_sem=send, recv_sem=recv, device_id=to, device_id_type=MESH
-        )
-        copy.start()
-        return copy
-
-    def mine(to):
-        return maps_ref.at[:, pl.ds(pl.multiple_of(to * columns, 128), columns)]
-
-    locals_ = [
-        pltpu.make_async_copy(mine(w), back_ref.at[p, w], local_sem.at[0]),
-        pltpu.make_async_copy(pairs_ref.at[w], back_pair_ref.at[p, w], local_sem.at[1]),
-        pltpu.make_async_copy(ids_ref, all_ids_ref.at[p], local_sem.at[2]),
-    ]
-    for copy in locals_:
-        copy.start()
-    parts = []
-    for k in range(1, n):
-        to = lax.rem(w + k, n)
-        parts.append((
-            remote(mine(to), back_ref.at[p, w], part_send.at[0, k], part_recv.at[0, k], (p, to)),
-            remote(pairs_ref.at[to], back_pair_ref.at[p, w], part_send.at[1, k], part_recv.at[1, k], (p, to)),
-        ))
-    far = [
-        remote(ids_ref, all_ids_ref.at[p], ids_send.at[k], ids_recv.at[k], (lax.rem(p + k, groups), w))
-        for k in range(1, groups)
-    ]
-
-    def pass_on(owner, slot, source, source_pair):
-        for k in range(1, groups):
-            to = (lax.rem(p + k, groups), w)
-            far.append(
-                remote(source, back_ref.at[p, owner], far_send.at[0, k, slot], far_recv.at[0, k, slot], to)
-            )
-            far.append(
-                remote(source_pair, back_pair_ref.at[p, owner], far_send.at[1, k, slot], far_recv.at[1, k, slot], to)
-            )
-
-    pass_on(w, 0, mine(w), pairs_ref.at[w])
-    for k in range(1, n):
-        owner = lax.rem(w - k + n, n)
-        parts[k - 1][0].wait_recv()
-        parts[k - 1][1].wait_recv()
-        pass_on(owner, k, back_ref.at[p, owner], back_pair_ref.at[p, owner])
-    for pair in parts:
-        for copy in pair:
-            copy.wait_send()
-    for copy in far:
-        copy.wait_send()
-        copy.wait_recv()
-    for copy in locals_:
-        copy.wait()
-
-
-def spread(groups, n, maps, pairs, ids):
-    map_rows, width = maps.shape
-    columns = width // n
-    any_spec = pl.BlockSpec(memory_space=pl.ANY)
-    return pl.pallas_call(
-        functools.partial(spread_kernel, groups, n),
-        out_shape=(
-            jax.ShapeDtypeStruct((groups, n, map_rows, columns), jnp.bfloat16),
-            jax.ShapeDtypeStruct((groups,) + pairs.shape, jnp.bfloat16),
-            jax.ShapeDtypeStruct((groups,) + ids.shape, jnp.int32),
-        ),
-        in_specs=[any_spec] * 3,
-        out_specs=(any_spec,) * 3,
-        scratch_shapes=[
-            pltpu.SemaphoreType.DMA((3,)),
-            pltpu.SemaphoreType.DMA((2, n)),
-            pltpu.SemaphoreType.DMA((2, n)),
-            pltpu.SemaphoreType.DMA((2, groups, n)),
-            pltpu.SemaphoreType.DMA((2, groups, n)),
-            pltpu.SemaphoreType.DMA((groups,)),
-            pltpu.SemaphoreType.DMA((groups,)),
-        ],
-        compiler_params=pltpu.CompilerParams(collective_id=1, has_side_effects=True),
-    )(maps, pairs, ids)
-
-
-PIECES = 4
+PIECES = 2
 PIECE_HEADS = KV_HEADS // PIECES
 PIECE_WIDTH = PIECE_HEADS * HEAD_DIM
 
 
-def block_kernel(n, end_ref, x_ref, query_ref, own_ref, cotangent_ref, context_cotangent_ref,
-                 send_down_ref, send_up_ref, send_pair_ref, prompt_ref, grads_ref, pair_grads_ref,
+def block_kernel(groups, n, end_ref, x_in, query_in, own_in, cotangent_in, context_cotangent_in,
+                 send_down_ref, send_up_ref, send_pair_ref, prompt_ref, ids_ref,
+                 back_ref, back_pair_ref, all_ids_ref,
+                 x_ref, query_ref, own_ref, cotangent_ref, context_cotangent_ref,
+                 grads_ref, pair_grads_ref,
                  maps_ref, pairs_ref, rows_ref, low_t, low, up_out, up_out_t, sums,
-                 local_sem, own_sem, ring_send, ring_recv, core_send, core_recv, part_send, part_recv):
+                 local_sem, own_sem, ring_send, ring_recv, core_send, core_recv, part_send, part_recv,
+                 load_sem, stay_sem, ids_send, ids_recv, early_send, early_recv, early_far_send, early_far_recv,
+                 late_send, late_recv, late_far_send, late_far_recv):
     p = lax.axis_index("prompt")
     w = lax.axis_index("wide")
     chips = n // 2
@@ -155,7 +66,18 @@
     barrier = pltpu.get_barrier_semaphore()
     for k in range(1, n):
         pl.semaphore_signal(barrier, inc=1, device_id=(p, lax.rem(w + k, n)), device_id_type=MESH)
-    pl.semaphore_wait(barrier, n - 1)
+    for k in range(1, groups):
+        pl.semaphore_signal(barrier, inc=1, device_id=(lax.rem(p + k, groups), w), device_id_type=MESH)
+    loads = [
+        pltpu.make_async_copy(src, dst, load_sem.at[i])
+        for i, (src, dst) in enumerate((
+            (x_in, x_ref), (cotangent_in, cotangent_ref), (query_in, query_ref), (own_in, own_ref),
+            (context_cotangent_in, context_cotangent_ref),
+        ))
+    ]
+    for copy in loads:
+        copy.start()
+    pl.semaphore_wait(barrier, n + groups - 2)
 
     def shard(offset):
         return 2 * chip_at(place + offset, chips) + core
@@ -211,6 +133,69 @@
         across(piece, 2 * step - 1).start()
         if step < half:
             across(piece, 2 * step).start()
+
+    def send_far(k, src, dst, send, recv):
+        return pltpu.make_async_remote_copy(
+            src_ref=src, dst_ref=dst, send_sem=send, recv_sem=recv,
+            device_id=(lax.rem(p + k, groups), w), device_id_type=MESH,
+        )
+
+    owners = n // KV_HEADS
+    first_head = w // owners
+
+    def columns_of(owner):
+        return pl.ds(pl.multiple_of(owner * map_columns, 128), map_columns)
+
+    def early(owner):
+        return (
+            remote(grads_ref.at[64:96, columns_of(owner)], back_ref.at[p, w, 64:96],
+                   early_send.at[0, owner], early_recv.at[0, w], owner),
+            remote(pair_grads_ref.at[owner], back_pair_ref.at[p, w],
+                   early_send.at[1, owner], early_recv.at[1, w], owner),
+        )
+
+    def early_from(source):
+        return (
+            remote(grads_ref.at[64:96, columns_of(w)], back_ref.at[p, source, 64:96],
+                   early_send.at[0, source], early_recv.at[0, source], source),
+            remote(pair_grads_ref.at[w], back_pair_ref.at[p, source],
+                   early_send.at[1, source], early_recv.at[1, source], source),
+        )
+
+    def early_far(k, source, own):
+        src = grads_ref.at[64:96, columns_of(w)] if own else back_ref.at[p, source, 64:96]
+        src_pair = pair_grads_ref.at[w] if own else back_pair_ref.at[p, source]
+        return (
+            send_far(k, src, back_ref.at[p, source, 64:96],
+                     early_far_send.at[0, k, source], early_far_recv.at[0, k, source]),
+            send_far(k, src_pair, back_pair_ref.at[p, source],
+                     early_far_send.at[1, k, source], early_far_recv.at[1, k, source]),
+        )
+
+    def stay_early():
+        return (
+            pltpu.make_async_copy(grads_ref.at[64:96, columns_of(w)], back_ref.at[p, w, 64:96], stay_sem.at[0]),
+            pltpu.make_async_copy(pair_grads_ref.at[w], back_pair_ref.at[p, w], stay_sem.at[1]),
+        )
+
+    def forward_early():
+        def one(offset, carry):
+            source = lax.rem(w + offset, n)
+            for copy in early_from(source):
+                copy.wait_recv()
+            for k in range(1, groups):
+                for copy in early_far(k, source, False):
+                    copy.start()
+            return carry
+
+        lax.fori_loop(1, n, one, 0)
+
+    id_copies = [
+        send_far(k, ids_ref, all_ids_ref.at[p], ids_send.at[k], ids_recv.at[k]) for k in range(1, groups)
+    ]
+    id_copies.append(pltpu.make_async_copy(ids_ref, all_ids_ref.at[p], stay_sem.at[3]))
+    for copy in id_copies:
+        copy.start()
 
     part_columns = pl.ds(pl.multiple_of(w * map_columns, 128), map_columns)
     down_here = maps_ref.at[0:64, part_columns]
@@ -240,6 +225,9 @@
         copy.wait()
     for copy in parts:
         copy.wait_recv()
+
+    for copy in loads:
+        copy.wait()
 
     inverse_root = HEAD_DIM ** (-0.5)
     pair_columns = pairs_ref.shape[2]
@@ -338,8 +326,8 @@
         sums[16:32, :] += dot(up_pair[0:16], key_grad, NT)
         sums[32:48, :] += dot(up_pair[16:32], value_grad, NT)
         sums[48:64, :] += dot(down_out, context, NT)
-        grads_ref[48:64, columns] = dot(up_out[...], context).astype(jnp.bfloat16)
-        grads_ref[64:80, columns] = (adapter_scale * dot(low[0:16, :], query_grad)).astype(jnp.bfloat16)
+        grads_ref[64:80, columns] = dot(up_out[...], context).astype(jnp.bfloat16)
+        grads_ref[80:96, columns] = (adapter_scale * dot(low[0:16, :], query_grad)).astype(jnp.bfloat16)
         pair_grad = jnp.concatenate(
             [dot(low[16:32, :], key_grad), dot(low[32:48, :], value_grad)], axis=0
         ) * adapter_scale
@@ -348,6 +336,26 @@
             pair_grads_ref[head * lanes + i] = pair_grad[:, i * pair_columns:(i + 1) * pair_columns]
 
 
+        for i in range(owners):
+            owner = head * owners + i
+
+            @pl.when(owner != w)
+            def _():
+                for copy in early(owner):
+                    copy.start()
+
+            @pl.when(owner == w)
+            def _():
+                for copy in stay_early():
+                    copy.start()
+                for k in range(1, groups):
+                    for copy in early_far(k, w, True):
+                        copy.start()
+
+        @pl.when(head == first_head + 1)
+        def _():
+            forward_early()
+
         following = piece + 1
         for turn in range(PIECE_HEADS):
             @pl.when((inner == turn) & (following < PIECES))
@@ -366,10 +374,64 @@
     up_low = (adapter_scale * sums[0:48, :]).astype(jnp.bfloat16)
     out_low = sums[48:64, :].astype(jnp.bfloat16)
     grads_ref[0:48, :] = dot(up_low, x_ref[...]).astype(jnp.bfloat16)
-    grads_ref[80:96, :] = (adapter_scale * dot(out_low, cotangent_ref[...])).astype(jnp.bfloat16)
-
-    for copy in parts:
+    grads_ref[48:64, :] = (adapter_scale * dot(out_low, cotangent_ref[...])).astype(jnp.bfloat16)
+
+    late = []
+    for k in range(1, n):
+        to = lax.rem(w + k, n)
+        copy = remote(
+            grads_ref.at[0:64, columns_of(to)], back_ref.at[p, w, 0:64], late_send.at[k], late_recv.at[k], to
+        )
+        copy.start()
+        late.append(copy)
+    stay = pltpu.make_async_copy(grads_ref.at[0:64, columns_of(w)], back_ref.at[p, w, 0:64], stay_sem.at[2])
+    stay.start()
+    far = [
+        send_far(k, grads_ref.at[0:64, columns_of(w)], back_ref.at[p, w, 0:64],
+                 late_far_send.at[k, 0], late_far_recv.at[k, 0])
+        for k in range(1, groups)
+    ]
+    for copy in far:
+        copy.start()
+
+    @pl.when(first_head == KV_HEADS - 1)
+    def _():
+        forward_early()
+
+    for j in range(1, n):
+        source = lax.rem(w - j + n, n)
+        late[j - 1].wait_recv()
+        for k in range(1, groups):
+            here = back_ref.at[p, source, 0:64]
+            copy = send_far(k, here, here, late_far_send.at[k, j], late_far_recv.at[k, j])
+            copy.start()
+            far.append(copy)
+
+    for copy in late + parts:
         copy.wait_send()
+    for copy in stay_early():
+        copy.wait()
+    stay.wait()
+
+    def finish(offset, carry):
+        other = lax.rem(w + offset, n)
+        for copy in early(other):
+            copy.wait_send()
+        for k in range(1, groups):
+            for copy in early_far(k, other, False):
+                copy.wait_send()
+                copy.wait_recv()
+        return carry
+
+    lax.fori_loop(1, n, finish, 0)
+    for k in range(1, groups):
+        for copy in early_far(k, w, True):
+            copy.wait_send()
+            copy.wait_recv()
+    for copy in far + id_copies[:-1]:
+        copy.wait_send()
+        copy.wait_recv()
+    id_copies[-1].wait()
     for piece in range(PIECES):
         for step in range(1, half + 1):
             for direction in range(2):
@@ -378,22 +440,30 @@
             across(piece, slot).wait_send()
 
 
-def block_gradients(n, end, x, query, own_pair, cotangent, context_cotangent, send_down, send_up, send_pair, prompt):
+def block_gradients(groups, n, end, x, query, own_pair, cotangent, context_cotangent, send_down, send_up, send_pair,
+                    prompt, ids):
     tokens, width = x.shape
     map_rows = send_down.shape[1] + send_up.shape[1]
     chips = n // 2
     steps = chips // 2 + 1
     any_spec = pl.BlockSpec(memory_space=pl.ANY)
-    vmem = pl.BlockSpec(memory_space=pltpu.VMEM)
     return pl.pallas_call(
-        functools.partial(block_kernel, n),
+        functools.partial(block_kernel, groups, n),
         out_shape=(
-            jax.ShapeDtypeStruct((map_rows, width), jnp.bfloat16),
-            jax.ShapeDtypeStruct(send_pair.shape, jnp.bfloat16),
+            jax.ShapeDtypeStruct((groups, n, map_rows, width // n), jnp.bfloat16),
+            jax.ShapeDtypeStruct((groups,) + send_pair.shape, jnp.bfloat16),
+            jax.ShapeDtypeStruct((groups,) + ids.shape, jnp.int32),
         ),
-        in_specs=[pl.BlockSpec(memory_space=pltpu.SMEM)] + [vmem] * 5 + [any_spec] * 4,
-        out_specs=(vmem, vmem),
+        in_specs=[pl.BlockSpec(memory_space=pltpu.SMEM)] + [any_spec] * 10,
+        out_specs=(any_spec,) * 3,
         scratch_shapes=[
+            pltpu.VMEM(x.shape, jnp.bfloat16),
+            pltpu.VMEM(query.shape, jnp.bfloat16),
+            pltpu.VMEM(own_pair.shape, jnp.bfloat16),
+            pltpu.VMEM(cotangent.shape, jnp.bfloat16),
+            pltpu.VMEM(context_cotangent.shape, jnp.bfloat16),
+            pltpu.VMEM((map_rows, width), jnp.bfloat16),
+            pltpu.VMEM(send_pair.shape, jnp.bfloat16),
             pltpu.VMEM((map_rows, width), jnp.bfloat16),
             pltpu.VMEM(send_pair.shape, jnp.bfloat16),
             pltpu.VMEM((PIECES, n * prompt.shape[1], prompt.shape[2]), jnp.bfloat16),
@@ -410,11 +480,24 @@
             pltpu.SemaphoreType.DMA((PIECES, chips)),
             pltpu.SemaphoreType.DMA((3, n)),
             pltpu.SemaphoreType.DMA((3, n)),
+            pltpu.SemaphoreType.DMA((5,)),
+            pltpu.SemaphoreType.DMA((4,)),
+            pltpu.SemaphoreType.DMA((groups,)),
+            pltpu.SemaphoreType.DMA((groups,)),
+            pltpu.SemaphoreType.DMA((2, n)),
+            pltpu.SemaphoreType.DMA((2, n)),
+            pltpu.SemaphoreType.DMA((2, groups, n)),
+            pltpu.SemaphoreType.DMA((2, groups, n)),
+            pltpu.SemaphoreType.DMA((n,)),
+            pltpu.SemaphoreType.DMA((n,)),
+            pltpu.SemaphoreType.DMA((groups, n)),
+            pltpu.SemaphoreType.DMA((groups, n)),
         ],
         compiler_params=pltpu.CompilerParams(
             collective_id=0, has_side_effects=True, vmem_limit_bytes=48 * 1024 * 1024
         ),
-    )(end, x, query, own_pair, cotangent, context_cotangent, send_down, send_up, send_pair, prompt)
+    )(end, x, query, own_pair, cotangent, context_cotangent, send_down, send_up, send_pair, prompt,
+      ids)
 
 
 def total_kernel(groups, n, ids_ref, back_ref, back_pair_ref, down_ref, up_ref, pair_ref):
@@ -424,10 +507,11 @@
     for group in range(groups):
         def step(source, carry):
             adapter = ids_ref[group, 0, source]
-            for part in range(4):
-                down_ref[adapter, part] += back_ref[group, source, 16 * part:16 * (part + 1)].astype(jnp.float32)
+            for part, start in enumerate((0, 16, 32, 64)):
+                down_ref[adapter, part] += back_ref[group, source, start:start + 16].astype(jnp.float32)
+            for part, start in enumerate((80, 48)):
+                up_ref[adapter, part] += back_ref[group, source, start:start + 16].astype(jnp.float32)
             for part in range(2):
-                up_ref[adapter, part] += back_ref[group, source, 64 + 16 * part:80 + 16 * part].astype(jnp.float32)
                 pair_ref[adapter, part] += back_pair_ref[group, source, 16 * part:16 * (part + 1)].astype(jnp.float32)
             return carry
 
@@ -473,11 +557,11 @@
     prompt = jnp.transpose(
         prompt_key_value[0].reshape(rows, 2, PIECES, PIECE_WIDTH), (2, 0, 1, 3)
     ).reshape(PIECES, rows, 2 * PIECE_WIDTH)
-    grads, pair_grads = block_gradients(
-        n, prompt_block_end, candidate_hidden[0], frozen_query[0], candidate_key_value[0],
+    back, back_pair, all_ids = block_gradients(
+        groups, n, prompt_block_end, candidate_hidden[0], frozen_query[0], candidate_key_value[0],
         output_cotangent[0], context_cotangent[0], send_down, send_up, send_pair, prompt,
+        candidate_adapter,
     )
-    back, back_pair, all_ids = spread(groups, n, grads, pair_grads, candidate_adapter)
     return totals(all_ids, back, back_pair)
 
 

time: 143 us -> 119 us (0.83)
  Pallas kernels: 128 us -> 105 us
    pallas_call x2 -> x1, Pallas kernels: 125 us -> 102 us  [block_gradients(): pl.pallas_call(functools.partial(block_kernel, groups, n), out_shape=(jax...]
    unnamed x20 -> x18, local copies, waits for them, and re-layouts: 7 us -> 5.86 us
where the time goes in v3:
time: 119 us; the launch traced here: 118 us
  Pallas kernels  105 us (88%)
  local copies, waits for them, and re-layouts  11.8 us (10%)
  between operations  1.45 us (1%)
    pallas_call x1, Pallas kernels, block_gradients(): pl.pallas_call(functools.partial(block_kernel, groups, n), out_shape=(jax...  102 us
    unnamed x18, local copies, waits for them, and re-layouts  5.86 us

profile of v3, /device:TPU:24, one launch (start us, length us, event | category | flops | bytes accessed | tf_op | source)
XLA Modules:
  0.0 118.4 jit_solution(13570689108407124679)
XLA Ops:
  0.6 0.0 copy-start
  1.3 0.7 fusion
  2.0 1.5 %gather_fusion.2 = bf16[16,2,16,64]{3,2,1,0:T(8,128)(2,1)S(1)} fusion(bf16[16,2,16,64]{3,2,1,0:T(8,128)(2,1)} %param.19, s32[1024]{0:T(1024)S(1)} %pad_clamp_fusion), kind=kCustom, calls=%fused_computation.2 | custom fusion | bytes 131136 | tf_op jit(solution)/shard_map/gather | solution.py:555
  3.5 0.0 copy-start.2
  3.5 0.0 copy-start.3
  3.5 0.0 copy-start.8
  3.5 1.7 %gather_fusion.1 = bf16[16,2,16,256]{3,2,1,0:T(8,128)(2,1)S(1)} fusion(bf16[16,2,16,256]{3,2,1,0:T(8,128)(2,1)} %param.18, s32[1024]{0:T(1024)S(1)} %pad_clamp_fusion), kind=kCustom, calls=%fused_computation.1 | custom fusion | bytes 524352 | tf_op jit(solution)/shard_map/gather | solution.py:554
  5.2 1.1 reshape_squeeze.3
  6.4 0.2 copy.16
  6.6 0.9 reshape.49.prompt_ref
  7.4 0.0 copy-done
  7.4 0.6 gather_fusion
  8.0 0.0 copy-done.2
  8.0 0.0 copy-done.3
  8.0 0.0 copy-done.8
  8.1 0.0 copy-start.4
  8.1 1.2 %copy-done.4 = bf16[1,128,4096]{2,1,0:T(8,128)(2,1)S(1)} copy-done((bf16[1,128,4096]{2,1,0:T(8,128)(2,1)S(1)}, bf16[1,128,4096]{2,1,0:T(8,128)(2,1)}, u32[]{:S(2)}) %copy-start.4) | copy-done | bytes 1048600
  9.3 1.2 %copy-done.5 = bf16[1,128,4096]{2,1,0:T(8,128)(2,1)S(1)} copy-done((bf16[1,128,4096]{2,1,0:T(8,128)(2,1)S(1)}, bf16[1,128,4096]{2,1,0:T(8,128)(2,1)}, u32[]{:S(2)}) %copy-start.5) | copy-done | bytes 1048600
  10.5 0.9 copy-done.6
  11.5 1.0 copy-done.7
  12.5 102.2 %shard_map.130 = (bf16[2,16,96,256]{3,2,1,0:T(8,128)(2,1)}, bf16[2,16,32,64]{3,2,1,0:T(8,128)(2,1)S(1)}, s32[2,1,16]{2,1,0:T(1,128)S(1)}) custom-call(s32[1,1]{1,0:T(1,128)S(6)} %copy.17.end_ref, bf16[128,4096]{1,0:T(8,128)(2,1)S(1)} %bitcast.16, bf16[128,4096]{1,0:T(8,128)(2,1)S(1)} %bitcast.17, bf16[128,2048]{1,0:T(8,128)(2,1)S(1)} %bitcast.21, ...), custom_call_target="tpu_custom_call" | custom-call | tf_op jit(solution)/shard_map/pallas_call | solution.py:450
  114.7 0.0 copy-start.1
  114.7 1.4 %copy-done.1 = bf16[2,16,96,256]{3,2,1,0:T(8,128)(2,1)S(1)} copy-done((bf16[2,16,96,256]{3,2,1,0:T(8,128)(2,1)S(1)}, bf16[2,16,96,256]{3,2,1,0:T(8,128)(2,1)}, u32[]{:S(2)}) %copy-start.1) | copy-done | bytes 1572888
  116.1 2.4 %shard_map.131 = (f32[16,4,16,256]{3,2,1,0:T(8,128)}, f32[16,2,16,256]{3,2,1,0:T(8,128)}, f32[16,2,16,64]{3,2,1,0:T(8,128)}) custom-call(s32[2,1,16]{2,1,0:T(1,128)S(1)} %get-tuple-element.6.ids_ref, bf16[2,16,96,256]{3,2,1,0:T(8,128)(2,1)S(1)} %copy-done.1, bf16[2,16,32,64]{3,2,1,0:T(8,128)(2,1)S(1)} %get-tuple-element.8.back_pair_ref), custom_call_target="tpu_custom_call" | custom-call | tf_op jit(solution)/shard_map/pallas_call | solution.py:524
  (4 shorter events, 0.0 us)
Async XLA Ops:
  0.6 6.8 %copy-start = (bf16[16,4,16,256]{3,2,1,0:T(8,128)(2,1)S(1)}, bf16[16,4,16,256]{3,2,1,0:T(8,128)(2,1)}, u32[]{:S(2)}) copy-start(bf16[16,4,16,256]{3,2,1,0:T(8,128)(2,1)} %param.17) | copy-start | bytes 1572868
  3.5 4.5 %copy-start.2 = (bf16[1,128,4096]{2,1,0:T(8,128)(2,1)S(1)}, bf16[1,128,4096]{2,1,0:T(8,128)(2,1)}, u32[]{:S(2)}) copy-start(bf16[1,128,4096]{2,1,0:T(8,128)(2,1)} %param.11) | copy-start | bytes 3145732
  3.5 4.5 %copy-start.3 = (bf16[1,128,4096]{2,1,0:T(8,128)(2,1)S(1)}, bf16[1,128,4096]{2,1,0:T(8,128)(2,1)}, u32[]{:S(2)}) copy-start(bf16[1,128,4096]{2,1,0:T(8,128)(2,1)} %param.12) | copy-start | bytes 3145732
  3.5 4.5 %copy-start.8 = (s32[1,16]{1,0:T(1,128)S(1)}, s32[1,16]{1,0:T(1,128)}, u32[]{:S(2)}) copy-start(s32[1,16]{1,0:T(1,128)} %ids_ref.1) | copy-start | bytes 196
  8.1 1.2 %copy-start.4 = (bf16[1,128,4096]{2,1,0:T(8,128)(2,1)S(1)}, bf16[1,128,4096]{2,1,0:T(8,128)(2,1)}, u32[]{:S(2)}) copy-start(bf16[1,128,4096]{2,1,0:T(8,128)(2,1)} %param.20) | copy-start | bytes 3145732
  9.3 1.2 %copy-start.5 = (bf16[1,128,4096]{2,1,0:T(8,128)(2,1)S(1)}, bf16[1,128,4096]{2,1,0:T(8,128)(2,1)}, u32[]{:S(2)}) copy-start(bf16[1,128,4096]{2,1,0:T(8,128)(2,1)} %param.21) | copy-start | bytes 3145732
  10.5 0.9 copy-start.6
  11.5 1.0 copy-start.7
  114.7 1.4 %copy-start.1 = (bf16[2,16,96,256]{3,2,1,0:T(8,128)(2,1)S(1)}, bf16[2,16,96,256]{3,2,1,0:T(8,128)(2,1)}, u32[]{:S(2)}) copy-start(bf16[2,16,96,256]{3,2,1,0:T(8,128)(2,1)} %get-tuple-element.7.back_ref) | copy-start | bytes 4718596

commit v4 on v3

--- a/solution.py
+++ b/solution.py
@@ -454,7 +454,7 @@
             jax.ShapeDtypeStruct((groups,) + send_pair.shape, jnp.bfloat16),
             jax.ShapeDtypeStruct((groups,) + ids.shape, jnp.int32),
         ),
-        in_specs=[pl.BlockSpec(memory_space=pltpu.SMEM)] + [any_spec] * 10,
+        in_specs=[pl.BlockSpec(memory_space=pltpu.SMEM)] + [pl.BlockSpec(memory_space=pltpu.HBM)] * 5 + [any_spec] * 5,
         out_specs=(any_spec,) * 3,
         scratch_shapes=[
             pltpu.VMEM(x.shape, jnp.bfloat16),

time: 119 us -> 119 us (level)
  no operation moved by 1% of the time
where the time goes in v4:
time: 119 us; the launch traced here: 118 us
  Pallas kernels  105 us (88%)
  local copies, waits for them, and re-layouts  11.8 us (10%)
  between operations  1.45 us (1%)
    pallas_call x1, Pallas kernels, block_gradients(): pl.pallas_call(functools.partial(block_kernel, groups, n), out_shape=(jax...  102 us
    unnamed x18, local copies, waits for them, and re-layouts  5.86 us

profile of v4, /device:TPU:24, one launch (start us, length us, event | category | flops | bytes accessed | tf_op | source)
XLA Modules:
  0.0 118.4 jit_solution(13570689108407124679)
XLA Ops:
  0.6 0.0 copy-start
  1.3 0.7 fusion
  2.0 1.5 %gather_fusion.2 = bf16[16,2,16,64]{3,2,1,0:T(8,128)(2,1)S(1)} fusion(bf16[16,2,16,64]{3,2,1,0:T(8,128)(2,1)} %param.19, s32[1024]{0:T(1024)S(1)} %pad_clamp_fusion), kind=kCustom, calls=%fused_computation.2 | custom fusion | bytes 131136 | tf_op jit(solution)/shard_map/gather | solution.py:555
  3.5 0.0 copy-start.2
  3.5 0.0 copy-start.3
  3.5 0.0 copy-start.8
  3.5 1.7 %gather_fusion.1 = bf16[16,2,16,256]{3,2,1,0:T(8,128)(2,1)S(1)} fusion(bf16[16,2,16,256]{3,2,1,0:T(8,128)(2,1)} %param.18, s32[1024]{0:T(1024)S(1)} %pad_clamp_fusion), kind=kCustom, calls=%fused_computation.1 | custom fusion | bytes 524352 | tf_op jit(solution)/shard_map/gather | solution.py:554
  5.2 1.1 reshape_squeeze.3
  6.4 0.2 copy.16
  6.6 0.9 reshape.49.prompt_ref
  7.4 0.0 copy-done
  7.4 0.6 gather_fusion
  8.0 0.0 copy-done.2
  8.0 0.0 copy-done.3
  8.0 0.0 copy-done.8
  8.1 0.0 copy-start.4
  8.1 1.2 %copy-done.4 = bf16[1,128,4096]{2,1,0:T(8,128)(2,1)S(1)} copy-done((bf16[1,128,4096]{2,1,0:T(8,128)(2,1)S(1)}, bf16[1,128,4096]{2,1,0:T(8,128)(2,1)}, u32[]{:S(2)}) %copy-start.4) | copy-done | bytes 1048600
  9.3 1.2 %copy-done.5 = bf16[1,128,4096]{2,1,0:T(8,128)(2,1)S(1)} copy-done((bf16[1,128,4096]{2,1,0:T(8,128)(2,1)S(1)}, bf16[1,128,4096]{2,1,0:T(8,128)(2,1)}, u32[]{:S(2)}) %copy-start.5) | copy-done | bytes 1048600
  10.5 0.9 copy-done.6
  11.5 1.0 copy-done.7
  12.5 102.2 %shard_map.130 = (bf16[2,16,96,256]{3,2,1,0:T(8,128)(2,1)}, bf16[2,16,32,64]{3,2,1,0:T(8,128)(2,1)S(1)}, s32[2,1,16]{2,1,0:T(1,128)S(1)}) custom-call(s32[1,1]{1,0:T(1,128)S(6)} %copy.17.end_ref, bf16[128,4096]{1,0:T(8,128)(2,1)S(1)} %bitcast.16, bf16[128,4096]{1,0:T(8,128)(2,1)S(1)} %bitcast.17, bf16[128,2048]{1,0:T(8,128)(2,1)S(1)} %bitcast.21, ...), custom_call_target="tpu_custom_call" | custom-call | tf_op jit(solution)/shard_map/pallas_call | solution.py:450
  114.7 0.0 copy-start.1
  114.7 1.4 %copy-done.1 = bf16[2,16,96,256]{3,2,1,0:T(8,128)(2,1)S(1)} copy-done((bf16[2,16,96,256]{3,2,1,0:T(8,128)(2,1)S(1)}, bf16[2,16,96,256]{3,2,1,0:T(8,128)(2,1)}, u32[]{:S(2)}) %copy-start.1) | copy-done | bytes 1572888
  116.1 2.4 %shard_map.131 = (f32[16,4,16,256]{3,2,1,0:T(8,128)}, f32[16,2,16,256]{3,2,1,0:T(8,128)}, f32[16,2,16,64]{3,2,1,0:T(8,128)}) custom-call(s32[2,1,16]{2,1,0:T(1,128)S(1)} %get-tuple-element.6.ids_ref, bf16[2,16,96,256]{3,2,1,0:T(8,128)(2,1)S(1)} %copy-done.1, bf16[2,16,32,64]{3,2,1,0:T(8,128)(2,1)S(1)} %get-tuple-element.8.back_pair_ref), custom_call_target="tpu_custom_call" | custom-call | tf_op jit(solution)/shard_map/pallas_call | solution.py:524
  (4 shorter events, 0.0 us)
Async XLA Ops:
  0.6 6.8 %copy-start = (bf16[16,4,16,256]{3,2,1,0:T(8,128)(2,1)S(1)}, bf16[16,4,16,256]{3,2,1,0:T(8,128)(2,1)}, u32[]{:S(2)}) copy-start(bf16[16,4,16,256]{3,2,1,0:T(8,128)(2,1)} %param.17) | copy-start | bytes 1572868
  3.5 4.5 %copy-start.2 = (bf16[1,128,4096]{2,1,0:T(8,128)(2,1)S(1)}, bf16[1,128,4096]{2,1,0:T(8,128)(2,1)}, u32[]{:S(2)}) copy-start(bf16[1,128,4096]{2,1,0:T(8,128)(2,1)} %param.11) | copy-start | bytes 3145732
  3.5 4.5 %copy-start.3 = (bf16[1,128,4096]{2,1,0:T(8,128)(2,1)S(1)}, bf16[1,128,4096]{2,1,0:T(8,128)(2,1)}, u32[]{:S(2)}) copy-start(bf16[1,128,4096]{2,1,0:T(8,128)(2,1)} %param.12) | copy-start | bytes 3145732
  3.5 4.5 %copy-start.8 = (s32[1,16]{1,0:T(1,128)S(1)}, s32[1,16]{1,0:T(1,128)}, u32[]{:S(2)}) copy-start(s32[1,16]{1,0:T(1,128)} %ids_ref.1) | copy-start | bytes 196
  8.1 1.2 %copy-start.4 = (bf16[1,128,4096]{2,1,0:T(8,128)(2,1)S(1)}, bf16[1,128,4096]{2,1,0:T(8,128)(2,1)}, u32[]{:S(2)}) copy-start(bf16[1,128,4096]{2,1,0:T(8,128)(2,1)} %param.20) | copy-start | bytes 3145732
  9.3 1.2 %copy-start.5 = (bf16[1,128,4096]{2,1,0:T(8,128)(2,1)S(1)}, bf16[1,128,4096]{2,1,0:T(8,128)(2,1)}, u32[]{:S(2)}) copy-start(bf16[1,128,4096]{2,1,0:T(8,128)(2,1)} %param.21) | copy-start | bytes 3145732
  10.5 0.9 copy-start.6
  11.5 1.0 copy-start.7
  114.7 1.4 %copy-start.1 = (bf16[2,16,96,256]{3,2,1,0:T(8,128)(2,1)S(1)}, bf16[2,16,96,256]{3,2,1,0:T(8,128)(2,1)}, u32[]{:S(2)}) copy-start(bf16[2,16,96,256]{3,2,1,0:T(8,128)(2,1)} %get-tuple-element.7.back_ref) | copy-start | bytes 4718596
